TPU v7x, 128 devices: a whole 4x4x4 slice. The times are simulated.
128 devices in a mesh: lon: 8 (over x, z_lo), lat: 16 (over y, z_hi, core).
Axes of the slice: x: 4, y: 4, z: 4 (z_hi: 2, z_lo: 2; z = z_hi * 2 + z_lo), core: 2. Of those that a mesh axis runs over, the one named last changes fastest.
Arguments:
- fields: float32 [192, 192, 1, 512], P('lat', 'lon'), may hold values from -6 to 6
- cotangent: float32 [192, 192, 1, 512], P('lat', 'lon'), may hold values from -6 to 6
- encoder_gain: float32 [512], replicated, may hold values from 0.25 to 1.75
- encoder_query: bfloat16 [512, 512], replicated, may hold values from -0.25 to 0.25
- encoder_keyval: bfloat16 [512, 1024], replicated, may hold values from -0.25 to 0.25
- encoder_output: bfloat16 [512, 512], replicated, may hold values from -0.25 to 0.25
- encoder_scale: float32 [8], replicated, may hold values from 2 to 12
- merge_gain: float32 [2048], replicated, may hold values from 0.25 to 1.75
- merge_weight: bfloat16 [2048, 1024], replicated, may hold values from -0.125 to 0.125
- coarse_gain: float32 [1024], replicated, may hold values from 0.25 to 1.75
- coarse_query: bfloat16 [1024, 1024], replicated, may hold values from -0.1875 to 0.1875
- coarse_keyval: bfloat16 [1024, 2048], replicated, may hold values from -0.1875 to 0.1875
- coarse_output: bfloat16 [1024, 1024], replicated, may hold values from -0.1875 to 0.1875
- coarse_scale: float32 [16], replicated, may hold values from 2 to 12
- expand_gain: float32 [1024], replicated, may hold values from 0.25 to 1.75
- expand_weight: bfloat16 [1024, 2048], replicated, may hold values from -0.1875 to 0.1875
- decoder_gain: float32 [512], replicated, may hold values from 0.25 to 1.75
- decoder_query: bfloat16 [512, 512], replicated, may hold values from -0.25 to 0.25
- decoder_keyval: bfloat16 [512, 1024], replicated, may hold values from -0.25 to 0.25
- decoder_output: bfloat16 [512, 512], replicated, may hold values from -0.25 to 0.25
- decoder_scale: float32 [8], replicated, may hold values from 2 to 12
Outputs:
- output: float32 [192, 192, 1, 512], P('lat', 'lon')
- grad_fields: float32 [192, 192, 1, 512], P('lat', 'lon')
All inputs are finite; a program needn't handle non-finite values.
Results may differ from a plain program's by a relative error of at most 0.025.
Values may be sent and summed in bfloat16 or wider, within the bound.
A program may use at most 192 MiB of HBM per device.

v0:
```python
import jax
import jax.numpy as jnp
from jax import lax
from jax.sharding import PartitionSpec as P

WLAT = 6
WLON = 12


EPS = 1e-05


def with_halo(x, sides, width, wrap):
    for axis, dim in sides:
        devices, length = (lax.axis_size(axis), x.shape[dim])
        up = [(i, (i + 1) % devices) for i in range(devices if wrap else devices - 1)]
        down = [(j, i) for i, j in up]
        last = lax.slice_in_dim(x, length - width, length, axis=dim)
        leading = lax.slice_in_dim(x, 0, width, axis=dim)
        before = lax.ppermute(last, axis, up)
        after = lax.ppermute(leading, axis, down)
        x = jnp.concatenate([before, x, after], axis=dim)
    return x


def norm_round(tensor, scaling):
    average = jnp.mean(tensor, axis=-1, keepdims=True)
    centred = tensor - average
    spread = jnp.mean(centred * centred, axis=-1, keepdims=True)
    return (centred * lax.rsqrt(spread + EPS) * scaling).astype(jnp.bfloat16)


def project(normed, weight):
    flattened = normed.reshape(-1, normed.shape[-1])
    result = jnp.dot(flattened, weight, preferred_element_type=jnp.float32)
    return result.reshape(normed.shape[:-1] + (weight.shape[1],))


def unit_heads(tensor, head_count):
    shaped = tensor.astype(jnp.float32).reshape(
        tensor.shape[:-1] + (head_count, tensor.shape[-1] // head_count)
    )
    return (shaped * lax.rsqrt(jnp.sum(shaped * shaped, axis=-1, keepdims=True) + 1.0)).astype(
        jnp.bfloat16
    )


def to_windows(tensor):
    extent, across, levels, channels = tensor.shape
    shaped = tensor.reshape(extent // WLAT, WLAT, across // WLON, WLON, levels, channels)
    shaped = shaped.transpose(0, 2, 1, 3, 4, 5)
    return shaped.reshape(extent // WLAT, across // WLON, WLAT * WLON * levels, channels)


def from_windows(tensor, levels):
    band_count, sector_count, tokens, channels = tensor.shape
    shaped = tensor.reshape(band_count, sector_count, WLAT, WLON, levels, channels)
    shaped = shaped.transpose(0, 2, 1, 3, 4, 5)
    return shaped.reshape(band_count * WLAT, sector_count * WLON, levels, channels)


def attend(query, keyval, key_ok, scaling, head_count):
    channels = query.shape[-1]
    levels = query.shape[2]
    queries = unit_heads(to_windows(query), head_count)
    paired = to_windows(keyval)
    keys = unit_heads(paired[..., :channels], head_count)
    values = paired[..., channels:].reshape(
        paired.shape[:-1] + (head_count, channels // head_count)
    )
    valid = to_windows(jnp.broadcast_to(key_ok[:, None, None, None], query.shape[:3] + (1,)))[
        ..., 0
    ]
    scores = jnp.einsum("abqhd,abkhd->abhqk", queries, keys, preferred_element_type=jnp.float32)
    scores = scores * scaling[:, None, None]
    weights = jnp.exp(scores) * valid[:, :, None, None, :]
    probs = (weights / jnp.sum(weights, axis=-1, keepdims=True)).astype(jnp.bfloat16)
    mixed = jnp.einsum(
        "abhqk,abkhd->abqhd", probs, values, preferred_element_type=jnp.float32
    ).astype(jnp.bfloat16)
    return from_windows(mixed.reshape(mixed.shape[:3] + (channels,)), levels)


def extend_normed(tensor, band_half, sector_half):
    taller = with_halo(tensor, (("lat", 0),), band_half, False)
    return with_halo(taller, (("lon", 1),), sector_half, True)


def fold_normed(gradient, band_half, sector_half):
    edges = jnp.concatenate([gradient[:, :sector_half], gradient[:, -sector_half:]], axis=1)
    middle = gradient[:, sector_half:-sector_half]
    arrived = with_halo(edges.astype(jnp.bfloat16), (("lon", 1),), sector_half, True).astype(
        edges.dtype
    )
    middle = middle.at[:, :sector_half].add(arrived[:, :sector_half])
    middle = middle.at[:, -sector_half:].add(arrived[:, -sector_half:])
    edges = jnp.concatenate([middle[:band_half], middle[-band_half:]], axis=0)
    inner = middle[band_half:-band_half]
    arrived = with_halo(edges.astype(jnp.bfloat16), (("lat", 0),), band_half, False).astype(
        edges.dtype
    )
    inner = inner.at[:band_half].add(arrived[:band_half])
    return inner.at[-band_half:].add(arrived[-band_half:])


def block_forward(stream, scaling_gain, query_weight, keyval_weight, output_weight, logit_scale):
    head_count = logit_scale.shape[0]
    band_half = WLAT // 2
    sector_half = WLON // 2
    own_rows = stream.shape[0]
    own_cols = stream.shape[1]
    normed, pull_norm = jax.vjp(lambda tensor: norm_round(tensor, scaling_gain), stream)
    first_row = lax.axis_index("lat") * own_rows - band_half
    total_rows = own_rows * lax.axis_size("lat")
    position = first_row + jnp.arange(own_rows + 2 * band_half, dtype=jnp.int32)
    key_ok = ((position >= 0) & (position < total_rows)).astype(jnp.float32)

    def pair_project(tensor):
        return project(tensor, keyval_weight).astype(jnp.bfloat16)

    def core(normed_own, pairs_ext):
        query = project(normed_own, query_weight).astype(jnp.bfloat16)
        query_ext = jnp.pad(
            query, ((band_half, band_half), (sector_half, sector_half), (0, 0), (0, 0))
        )
        mixed = attend(query_ext, pairs_ext, key_ok, logit_scale, head_count)
        mixed = mixed[band_half : band_half + own_rows, sector_half : sector_half + own_cols]
        return project(mixed, output_weight)

    normed_ext = extend_normed(normed, band_half, sector_half)
    pairs_ext, pull_pairs = jax.vjp(pair_project, normed_ext)
    branch_out, pull_core = jax.vjp(core, normed, pairs_ext)
    result = stream + branch_out

    def backward(gradient):
        grad_normed, grad_pairs = pull_core(gradient)
        grad_ext = pull_pairs(grad_pairs)[0]
        grad_rest = fold_normed(grad_ext.astype(jnp.float32), band_half, sector_half)
        combined = (grad_normed.astype(jnp.float32) + grad_rest).astype(jnp.bfloat16)
        return gradient + pull_norm(combined)[0]

    return (result, backward)


def merge_patches(stream, scaling_gain, weight):
    extent, across, levels, channels = stream.shape
    grouped = stream.reshape(extent // 2, 2, across // 2, 2, levels, channels).transpose(
        0, 2, 4, 1, 3, 5
    )
    grouped = grouped.reshape(extent // 2, across // 2, levels, 4 * channels)
    return project(norm_round(grouped, scaling_gain), weight)


def expand_patches(coarse, scaling_gain, weight):
    spread_out = project(norm_round(coarse, scaling_gain), weight)
    extent, across, levels, channels = spread_out.shape
    fine_width = channels // 4
    shaped = spread_out.reshape(extent, across, levels, 2, 2, fine_width).transpose(
        0, 3, 1, 4, 2, 5
    )
    return shaped.reshape(2 * extent, 2 * across, levels, fine_width)


def shards(
    fields,
    cotangent,
    encoder_gain,
    encoder_query,
    encoder_keyval,
    encoder_output,
    encoder_scale,
    merge_gain,
    merge_weight,
    coarse_gain,
    coarse_query,
    coarse_keyval,
    coarse_output,
    coarse_scale,
    expand_gain,
    expand_weight,
    decoder_gain,
    decoder_query,
    decoder_keyval,
    decoder_output,
    decoder_scale,
):
    section_one, back_encoder = block_forward(
        fields, encoder_gain, encoder_query, encoder_keyval, encoder_output, encoder_scale
    )
    coarse_in, pull_merge = jax.vjp(
        lambda tensor: merge_patches(tensor, merge_gain, merge_weight), section_one
    )
    coarse_out, back_coarse = block_forward(
        coarse_in, coarse_gain, coarse_query, coarse_keyval, coarse_output, coarse_scale
    )
    expanded, pull_expand = jax.vjp(
        lambda tensor: expand_patches(tensor, expand_gain, expand_weight), coarse_out
    )
    skipped = section_one + expanded
    output, back_decoder = block_forward(
        skipped, decoder_gain, decoder_query, decoder_keyval, decoder_output, decoder_scale
    )
    grad_skipped = back_decoder(cotangent)
    grad_coarse_out = pull_expand(grad_skipped)[0]
    grad_coarse_in = back_coarse(grad_coarse_out)
    grad_section = pull_merge(grad_coarse_in)[0] + grad_skipped
    grad_fields = back_encoder(grad_section)
    return (output, grad_fields)


def solution(mesh):
    in_specs = (
        P("lat", "lon", None, None),
        P("lat", "lon", None, None),
        P(),
        P(),
        P(),
        P(),
        P(),
        P(),
        P(),
        P(),
        P(),
        P(),
        P(),
        P(),
        P(),
        P(),
        P(),
        P(),
        P(),
        P(),
        P(),
    )
    out_specs = (P("lat", "lon", None, None), P("lat", "lon", None, None))
    return jax.shard_map(shards, mesh=mesh, in_specs=in_specs, out_specs=out_specs, check_vma=False)
```

profile of v0, /device:TPU:1, one launch (start us, length us, event | category | flops | bytes accessed | tf_op | source)
XLA Modules:
  0.0 585.7 jit_solution(1984822285048735653)
XLA Ops:
  6.0 6.9 %collective-permute-start = (bf16[3,24,1,512]{3,1,0,2:T(8,128)(2,1)}, bf16[3,24,1,512]{3,1,0,2:T(8,128)(2,1)}, u32[]{:S(2)}, u32[]{:S(2)}) collective-permute-start(bf16[3,24,1,512]{3,1,0,2:T(8,128)(2,1)} %get-tuple-element.196), channel_id=1, source_target_pairs={{0,1},{1,2},{2,3},{3,4},{4,5},{5,6},{6,7},{7,8},{8,9},{9,10},{10,1... | collective-permute-start | bytes 221192 | tf_op jit(solution)/shard_map/ppermute | solution.py:20
  33.5 4.4 copy.446
  45.3 6.4 %copy.531 = bf16[2048,1024]{1,0:T(8,128)(2,1)} copy(bf16[2048,1024]{0,1:T(8,128)(2,1)} %bitcast.389) | data formatting | bytes 8388608 | tf_op jit(solution)/shard_map/reshape.1050
  51.7 3.4 convolution_convert_fusion.2
  61.4 3.4 reshape.1931
  72.9 4.0 fusion.44
  81.8 3.5 copy.449
  98.0 3.4 fusion.163
  106.7 5.7 collective-permute-start.4
  117.9 3.6 reshape.2006
  124.8 3.4 reshape.1991
  131.4 3.5 copy.457
  136.2 4.0 collective-permute-start.7
  144.7 4.8 fusion.14
  175.8 3.5 copy.462
  186.1 3.6 convolution_bitcast_fusion
  194.0 6.7 %collective-permute-start.8 = (bf16[3,24,1,512]{3,1,0,2:T(8,128)(2,1)}, bf16[3,24,1,512]{3,1,0,2:T(8,128)(2,1)}, u32[]{:S(2)}, u32[]{:S(2)}) collective-permute-start(bf16[3,24,1,512]{3,1,0,2:T(8,128)(2,1)} %get-tuple-element.194), channel_id=1, source_target_pairs={{0,1},{1,2},{2,3},{3,4},{4,5},{5,6},{6,7},{7,8},{8,9},{9,10},{10,1... | collective-permute-start | bytes 221192 | tf_op jit(solution)/shard_map/ppermute | solution.py:20
  204.3 3.7 reshape.2007
  220.1 3.6 collective-permute-start.11
  224.3 4.6 copy.470
  228.9 3.6 convolution_convert_fusion.1
  232.5 3.4 reshape.1950
  239.0 3.4 reshape.1951
  252.5 3.7 fusion.43
  271.8 3.7 fusion.24
  286.5 3.4 reshape.1965
  289.9 3.7 fusion.50
  300.8 3.5 copy.473
  317.7 3.4 copy.480
  331.6 3.6 collective-permute-start.13
  340.5 3.4 scatter-add.40
  350.8 9.2 %collective-permute-start.14 = (bf16[3,24,1,512]{3,1,0,2:T(8,128)(2,1)S(1)}, bf16[3,24,1,512]{3,1,0,2:T(8,128)(2,1)S(1)}, u32[]{:S(2)}, u32[]{:S(2)}) collective-permute-start(bf16[3,24,1,512]{3,1,0,2:T(8,128)(2,1)S(1)} %get-tuple-element.182), channel_id=1, source_target_pairs={{0,1},{1,2},{2,3},{3,4},{4,5},{5,6},{6,7},{7,8},{8,9},{9,10},{10,1... | collective-permute-start | bytes 221192 | tf_op jit(solution)/shard_map/ppermute | solution.py:20
  362.1 5.2 collective-permute-done.15
  372.3 4.4 fusion.65
  392.6 3.5 convolution_convert_fusion.14
  407.5 3.4 fusion.35
  417.4 3.5 copy.494
  437.2 4.1 convolution_convert_fusion.20
  442.1 3.6 collective-permute-start.17
  452.7 3.6 scatter-add.46
  458.3 3.6 scatter-add.49
  464.1 4.6 collective-permute-start.18
  470.7 5.5 collective-permute-done.19
  478.0 4.4 fusion.33
  501.1 3.4 copy.505
  550.2 3.6 collective-permute-start.21
  568.7 6.1 %collective-permute-start.22 = (bf16[3,24,1,512]{3,1,0,2:T(8,128)(2,1)S(1)}, bf16[3,24,1,512]{3,1,0,2:T(8,128)(2,1)S(1)}, u32[]{:S(2)}, u32[]{:S(2)}) collective-permute-start(bf16[3,24,1,512]{3,1,0,2:T(8,128)(2,1)S(1)} %get-tuple-element.180), channel_id=1, source_target_pairs={{0,1},{1,2},{2,3},{3,4},{4,5},{5,6},{6,7},{7,8},{8,9},{9,10},{10,1... | collective-permute-start | bytes 221192 | tf_op jit(solution)/shard_map/ppermute | solution.py:20
  576.8 5.2 collective-permute-done.23
  (539 shorter events, 380.7 us)
Async XLA Ops:
  0.6 183.7 %copy-start = (bf16[1024,1024]{1,0:T(8,128)(2,1)S(1)}, bf16[1024,1024]{1,0:T(8,128)(2,1)}, u32[]{:S(2)}) copy-start(bf16[1024,1024]{1,0:T(8,128)(2,1)} %param.57) | copy-start | bytes 6291460
  0.7 15.4 %copy-start.42 = (bf16[512,512]{1,0:T(8,128)(2,1)S(1)}, bf16[512,512]{1,0:T(8,128)(2,1)}, u32[]{:S(2)}) copy-start(bf16[512,512]{1,0:T(8,128)(2,1)} %param.48) | copy-start | bytes 1572868
  0.7 15.8 %copy-start.39 = (f32[12,24,1,512]{3,2,1,0:T(1,128)S(1)}, f32[12,24,1,512]{3,2,1,0:T(1,128)}, u32[]{:S(2)}) copy-start(f32[12,24,1,512]{3,2,1,0:T(1,128)} %param.46) | copy-start | bytes 1769476
  6.0 32.0 %collective-permute-start = (bf16[3,24,1,512]{3,1,0,2:T(8,128)(2,1)}, bf16[3,24,1,512]{3,1,0,2:T(8,128)(2,1)}, u32[]{:S(2)}, u32[]{:S(2)}) collective-permute-start(bf16[3,24,1,512]{3,1,0,2:T(8,128)(2,1)} %get-tuple-element.196), channel_id=1, source_target_pairs={{0,1},{1,2},{2,3},{3,4},{4,5},{5,6},{6,7},{7,8},{8,9},{9,10},{10,1... | collective-permute-start | bytes 221192 | tf_op jit(solution)/shard_map/ppermute | solution.py:20
  12.9 25.1 %collective-permute-start.1 = (bf16[3,24,1,512]{3,1,0,2:T(8,128)(2,1)}, bf16[3,24,1,512]{3,1,0,2:T(8,128)(2,1)}, u32[]{:S(2)}, u32[]{:S(2)}) collective-permute-start(bf16[3,24,1,512]{3,1,0,2:T(8,128)(2,1)} %get-tuple-element.197), channel_id=1, source_target_pairs={{1,0},{2,1},{3,2},{4,3},{5,4},{6,5},{7,6},{8,7},{9,8},{10,9},{11,1... | collective-permute-start | bytes 221192 | tf_op jit(solution)/shard_map/ppermute | solution.py:21
  18.3 59.2 %copy-start.89 = (f32[3,72]{1,0:T(4,128)}, f32[3,72]{1,0:T(4,128)S(1)}, u32[]{:S(2)}) copy-start(f32[3,72]{1,0:T(4,128)S(1)} %transpose.231) | copy-start | bytes 2596
  38.8 12.9 %collective-permute-start.2 = (bf16[18,6,1,512]{3,1,0,2:T(8,128)(2,1)S(1)}, bf16[18,6,1,512]{3,1,0,2:T(8,128)(2,1)S(1)}, u32[]{:S(2)}, u32[]{:S(2)}) collective-permute-start(bf16[18,6,1,512]{3,1,0,2:T(8,128)(2,1)S(1)} %get-tuple-element.190), channel_id=1, source_target_pairs={{0,16},{16,32},{32,48},{48,64},{64,80},{80,96},{96,112},{112,0},{1... | collective-permute-start | bytes 331784 | tf_op jit(solution)/shard_map/ppermute | solution.py:20
  39.6 12.1 %collective-permute-start.3 = (bf16[18,6,1,512]{3,1,0,2:T(8,128)(2,1)S(1)}, bf16[18,6,1,512]{3,1,0,2:T(8,128)(2,1)S(1)}, u32[]{:S(2)}, u32[]{:S(2)}) collective-permute-start(bf16[18,6,1,512]{3,1,0,2:T(8,128)(2,1)S(1)} %get-tuple-element.191), channel_id=1, source_target_pairs={{16,0},{32,16},{48,32},{64,48},{80,64},{96,80},{112,96},{0,112},{1... | collective-permute-start | bytes 331784 | tf_op jit(solution)/shard_map/ppermute | solution.py:21
  45.3 27.6 %copy-start.54 = (f32[3,3,72,8]{2,3,1,0:T(8,128)}, f32[3,3,72,8]{2,3,1,0:T(8,128)S(1)}, u32[]{:S(2)}) copy-start(f32[3,3,72,8]{2,3,1,0:T(8,128)S(1)} %copy.445) | copy-start | bytes 62212
  101.6 15.1 %copy-start.76 = (f32[6,12]{1,0:T(8,128)}, f32[6,12]{1,0:T(8,128)S(1)}, u32[]{:S(2)}) copy-start(f32[6,12]{1,0:T(8,128)S(1)} %div.216) | copy-start | bytes 868
  106.7 28.2 %collective-permute-start.4 = (bf16[3,12,1,1024]{3,1,0,2:T(8,128)(2,1)}, bf16[3,12,1,1024]{3,1,0,2:T(8,128)(2,1)}, u32[]{:S(2)}, u32[]{:S(2)}) collective-permute-start(bf16[3,12,1,1024]{3,1,0,2:T(8,128)(2,1)} %get-tuple-element.198), channel_id=1, source_target_pairs={{0,1},{1,2},{2,3},{3,4},{4,5},{5,6},{6,7},{7,8},{8,9},{9,10},{10,1... | collective-permute-start | bytes 221192 | tf_op jit(solution)/shard_map/ppermute | solution.py:20
  112.5 22.5 %collective-permute-start.5 = (bf16[3,12,1,1024]{3,1,0,2:T(8,128)(2,1)}, bf16[3,12,1,1024]{3,1,0,2:T(8,128)(2,1)}, u32[]{:S(2)}, u32[]{:S(2)}) collective-permute-start(bf16[3,12,1,1024]{3,1,0,2:T(8,128)(2,1)} %get-tuple-element.199), channel_id=1, source_target_pairs={{1,0},{2,1},{3,2},{4,3},{5,4},{6,5},{7,6},{8,7},{9,8},{10,9},{11,1... | collective-permute-start | bytes 221192 | tf_op jit(solution)/shard_map/ppermute | solution.py:21
  136.1 6.9 %collective-permute-start.6 = (bf16[12,6,1,1024]{3,1,0,2:T(8,128)(2,1)S(1)}, bf16[12,6,1,1024]{3,1,0,2:T(8,128)(2,1)S(1)}, u32[]{:S(2)}, u32[]{:S(2)}) collective-permute-start(bf16[12,6,1,1024]{3,1,0,2:T(8,128)(2,1)S(1)} %get-tuple-element.192), channel_id=1, source_target_pairs={{0,16},{16,32},{32,48},{48,64},{64,80},{80,96},{96,112},{112,0},{1... | collective-permute-start | bytes 442376 | tf_op jit(solution)/shard_map/ppermute | solution.py:20
  136.2 8.5 %collective-permute-start.7 = (bf16[12,6,1,1024]{3,1,0,2:T(8,128)(2,1)S(1)}, bf16[12,6,1,1024]{3,1,0,2:T(8,128)(2,1)S(1)}, u32[]{:S(2)}, u32[]{:S(2)}) collective-permute-start(bf16[12,6,1,1024]{3,1,0,2:T(8,128)(2,1)S(1)} %get-tuple-element.193), channel_id=1, source_target_pairs={{16,0},{32,16},{48,32},{64,48},{80,64},{96,80},{112,96},{0,112},{1... | collective-permute-start | bytes 442376 | tf_op jit(solution)/shard_map/ppermute | solution.py:21
  140.2 27.7 %copy-start.60 = (f32[2,2,72,16]{2,3,1,0:T(8,128)}, f32[2,2,72,16]{2,3,1,0:T(8,128)S(1)}, u32[]{:S(2)}) copy-start(f32[2,2,72,16]{2,3,1,0:T(8,128)S(1)} %add_rsqrt_fusion.5) | copy-start | bytes 55300
  171.3 52.4 %copy-start.64 = (f32[2,2,16,72]{3,2,1,0:T(8,128)}, f32[2,2,16,72]{3,2,1,0:T(8,128)S(1)}, u32[]{:S(2)}) copy-start(f32[2,2,16,72]{3,2,1,0:T(8,128)S(1)} %get-tuple-element.208) | copy-start | bytes 55300
  194.0 24.3 %collective-permute-start.8 = (bf16[3,24,1,512]{3,1,0,2:T(8,128)(2,1)}, bf16[3,24,1,512]{3,1,0,2:T(8,128)(2,1)}, u32[]{:S(2)}, u32[]{:S(2)}) collective-permute-start(bf16[3,24,1,512]{3,1,0,2:T(8,128)(2,1)} %get-tuple-element.194), channel_id=1, source_target_pairs={{0,1},{1,2},{2,3},{3,4},{4,5},{5,6},{6,7},{7,8},{8,9},{9,10},{10,1... | collective-permute-start | bytes 221192 | tf_op jit(solution)/shard_map/ppermute | solution.py:20
  200.7 17.7 %collective-permute-start.9 = (bf16[3,24,1,512]{3,1,0,2:T(8,128)(2,1)}, bf16[3,24,1,512]{3,1,0,2:T(8,128)(2,1)}, u32[]{:S(2)}, u32[]{:S(2)}) collective-permute-start(bf16[3,24,1,512]{3,1,0,2:T(8,128)(2,1)} %get-tuple-element.195), channel_id=1, source_target_pairs={{1,0},{2,1},{3,2},{4,3},{5,4},{6,5},{7,6},{8,7},{9,8},{10,9},{11,1... | collective-permute-start | bytes 221192 | tf_op jit(solution)/shard_map/ppermute | solution.py:21
  220.1 8.8 %collective-permute-start.10 = (bf16[18,6,1,512]{3,1,0,2:T(8,128)(2,1)}, bf16[18,6,1,512]{3,1,0,2:T(8,128)(2,1)}, u32[]{:S(2)}, u32[]{:S(2)}) collective-permute-start(bf16[18,6,1,512]{3,1,0,2:T(8,128)(2,1)} %get-tuple-element.188), channel_id=1, source_target_pairs={{0,16},{16,32},{32,48},{48,64},{64,80},{80,96},{96,112},{112,0},{1... | collective-permute-start | bytes 331784 | tf_op jit(solution)/shard_map/ppermute | solution.py:20
  220.1 8.8 %collective-permute-start.11 = (bf16[18,6,1,512]{3,1,0,2:T(8,128)(2,1)}, bf16[18,6,1,512]{3,1,0,2:T(8,128)(2,1)}, u32[]{:S(2)}, u32[]{:S(2)}) collective-permute-start(bf16[18,6,1,512]{3,1,0,2:T(8,128)(2,1)} %get-tuple-element.189), channel_id=1, source_target_pairs={{16,0},{32,16},{48,32},{64,48},{80,64},{96,80},{112,96},{0,112},{1... | collective-permute-start | bytes 331784 | tf_op jit(solution)/shard_map/ppermute | solution.py:21
  331.6 6.3 %collective-permute-start.12 = (bf16[18,6,1,512]{3,1,0,2:T(8,128)(2,1)}, bf16[18,6,1,512]{3,1,0,2:T(8,128)(2,1)S(1)}, u32[]{:S(2)}, u32[]{:S(2)}) collective-permute-start(bf16[18,6,1,512]{3,1,0,2:T(8,128)(2,1)} %get-tuple-element.172), channel_id=1, source_target_pairs={{0,16},{16,32},{32,48},{48,64},{64,80},{80,96},{96,112},{112,0},{1... | collective-permute-start | bytes 331784 | tf_op jit(solution)/shard_map/ppermute | solution.py:20
  331.6 6.3 %collective-permute-start.13 = (bf16[18,6,1,512]{3,1,0,2:T(8,128)(2,1)}, bf16[18,6,1,512]{3,1,0,2:T(8,128)(2,1)S(1)}, u32[]{:S(2)}, u32[]{:S(2)}) collective-permute-start(bf16[18,6,1,512]{3,1,0,2:T(8,128)(2,1)} %get-tuple-element.173), channel_id=1, source_target_pairs={{16,0},{32,16},{48,32},{64,48},{80,64},{96,80},{112,96},{0,112},{1... | collective-permute-start | bytes 331784 | tf_op jit(solution)/shard_map/ppermute | solution.py:21
  343.9 24.3 %copy-start.104 = (f32[512]{0:T(512)S(1)}, f32[512]{0:T(512)}, u32[]{:S(2)}) copy-start(f32[512]{0:T(512)} %param.61) | copy-start | bytes 6148
  348.6 19.6 %copy-start.48 = (bf16[288,512]{1,0:T(8,128)(2,1)S(1)}, bf16[288,512]{1,0:T(8,128)(2,1)}, u32[]{:S(2)}) copy-start(bf16[288,512]{1,0:T(8,128)(2,1)} %convolution_convert_fusion.22) | copy-start | bytes 884740
  348.7 19.8 %copy-start.87 = (f32[12,24]{1,0:T(8,128)S(1)}, f32[12,24]{1,0:T(8,128)}, u32[]{:S(2)}) copy-start(f32[12,24]{1,0:T(8,128)} %copy-done.86) | copy-start | bytes 3460
  350.8 18.0 %copy-start.40 = (f32[12,24,1,512]{3,2,1,0:T(1,128)S(1)}, f32[12,24,1,512]{3,2,1,0:T(1,128)}, u32[]{:S(2)}) copy-start(f32[12,24,1,512]{3,2,1,0:T(1,128)} %param.46) | copy-start | bytes 1769476
  350.8 11.2 %collective-permute-start.14 = (bf16[3,24,1,512]{3,1,0,2:T(8,128)(2,1)S(1)}, bf16[3,24,1,512]{3,1,0,2:T(8,128)(2,1)S(1)}, u32[]{:S(2)}, u32[]{:S(2)}) collective-permute-start(bf16[3,24,1,512]{3,1,0,2:T(8,128)(2,1)S(1)} %get-tuple-element.182), channel_id=1, source_target_pairs={{0,1},{1,2},{2,3},{3,4},{4,5},{5,6},{6,7},{7,8},{8,9},{9,10},{10,1... | collective-permute-start | bytes 221192 | tf_op jit(solution)/shard_map/ppermute | solution.py:20
  360.1 7.2 %collective-permute-start.15 = (bf16[3,24,1,512]{3,1,0,2:T(8,128)(2,1)S(1)}, bf16[3,24,1,512]{3,1,0,2:T(8,128)(2,1)S(1)}, u32[]{:S(2)}, u32[]{:S(2)}) collective-permute-start(bf16[3,24,1,512]{3,1,0,2:T(8,128)(2,1)S(1)} %get-tuple-element.183), channel_id=1, source_target_pairs={{1,0},{2,1},{3,2},{4,3},{5,4},{6,5},{7,6},{8,7},{9,8},{10,9},{11,1... | collective-permute-start | bytes 221192 | tf_op jit(solution)/shard_map/ppermute | solution.py:21
  442.1 8.5 %collective-permute-start.16 = (bf16[12,6,1,1024]{3,1,0,2:T(8,128)(2,1)}, bf16[12,6,1,1024]{3,1,0,2:T(8,128)(2,1)S(1)}, u32[]{:S(2)}, u32[]{:S(2)}) collective-permute-start(bf16[12,6,1,1024]{3,1,0,2:T(8,128)(2,1)} %get-tuple-element.186), channel_id=1, source_target_pairs={{0,16},{16,32},{32,48},{48,64},{64,80},{80,96},{96,112},{112,0},{1... | collective-permute-start | bytes 442376 | tf_op jit(solution)/shard_map/ppermute | solution.py:20
  442.1 8.5 %collective-permute-start.17 = (bf16[12,6,1,1024]{3,1,0,2:T(8,128)(2,1)}, bf16[12,6,1,1024]{3,1,0,2:T(8,128)(2,1)S(1)}, u32[]{:S(2)}, u32[]{:S(2)}) collective-permute-start(bf16[12,6,1,1024]{3,1,0,2:T(8,128)(2,1)} %get-tuple-element.187), channel_id=1, source_target_pairs={{16,0},{32,16},{48,32},{64,48},{80,64},{96,80},{112,96},{0,112},{1... | collective-permute-start | bytes 442376 | tf_op jit(solution)/shard_map/ppermute | solution.py:21
  458.3 18.9 %copy-start.22 = (f32[6,12,1,1024]{3,1,0,2:T(8,128)S(1)}, f32[6,12,1,1024]{3,1,0,2:T(8,128)}, u32[]{:S(2)}) copy-start(f32[6,12,1,1024]{3,1,0,2:T(8,128)} %copy-done.21) | copy-start | bytes 884740
  458.3 18.9 %copy-start.75 = (f32[1024]{0:T(1024)S(1)}, f32[1024]{0:T(1024)}, u32[]{:S(2)}) copy-start(f32[1024]{0:T(1024)} %param.54) | copy-start | bytes 12292
  458.3 18.9 %copy-start.77 = (f32[6,12]{1,0:T(8,128)S(1)}, f32[6,12]{1,0:T(8,128)}, u32[]{:S(2)}) copy-start(f32[6,12]{1,0:T(8,128)} %copy-done.76) | copy-start | bytes 868
  461.9 15.3 %copy-start.45 = (f32[6,12,1,1024]{3,1,0,2:T(8,128)S(1)}, f32[6,12,1,1024]{3,1,0,2:T(8,128)}, u32[]{:S(2)}) copy-start(f32[6,12,1,1024]{3,1,0,2:T(8,128)} %reshape.2000) | copy-start | bytes 884740
  461.9 15.5 %copy-start.102 = (f32[6,12]{1,0:T(8,128)S(1)}, f32[6,12]{1,0:T(8,128)}, u32[]{:S(2)}) copy-start(f32[6,12]{1,0:T(8,128)} %copy-done.101) | copy-start | bytes 868
  461.9 15.5 %copy-start.88 = (f32[6,12]{1,0:T(8,128)S(1)}, f32[6,12]{1,0:T(8,128)}, u32[]{:S(2)}) copy-start(f32[6,12]{1,0:T(8,128)} %rsqrt.126) | copy-start | bytes 868
  464.1 6.6 %collective-permute-start.18 = (bf16[3,12,1,1024]{3,1,0,2:T(8,128)(2,1)S(1)}, bf16[3,12,1,1024]{3,1,0,2:T(8,128)(2,1)S(1)}, u32[]{:S(2)}, u32[]{:S(2)}) collective-permute-start(bf16[3,12,1,1024]{3,1,0,2:T(8,128)(2,1)S(1)} %get-tuple-element.184), channel_id=1, source_target_pairs={{0,1},{1,2},{2,3},{3,4},{4,5},{5,6},{6,7},{7,8},{8,9},{9,10},{10,1... | collective-permute-start | bytes 221192 | tf_op jit(solution)/shard_map/ppermute | solution.py:20
  468.7 7.4 %collective-permute-start.19 = (bf16[3,12,1,1024]{3,1,0,2:T(8,128)(2,1)S(1)}, bf16[3,12,1,1024]{3,1,0,2:T(8,128)(2,1)S(1)}, u32[]{:S(2)}, u32[]{:S(2)}) collective-permute-start(bf16[3,12,1,1024]{3,1,0,2:T(8,128)(2,1)S(1)} %get-tuple-element.185), channel_id=1, source_target_pairs={{1,0},{2,1},{3,2},{4,3},{5,4},{6,5},{7,6},{8,7},{9,8},{10,9},{11,1... | collective-permute-start | bytes 221192 | tf_op jit(solution)/shard_map/ppermute | solution.py:21
  550.2 6.4 %collective-permute-start.20 = (bf16[18,6,1,512]{3,1,0,2:T(8,128)(2,1)}, bf16[18,6,1,512]{3,1,0,2:T(8,128)(2,1)S(1)}, u32[]{:S(2)}, u32[]{:S(2)}) collective-permute-start(bf16[18,6,1,512]{3,1,0,2:T(8,128)(2,1)} %get-tuple-element.170), channel_id=1, source_target_pairs={{0,16},{16,32},{32,48},{48,64},{64,80},{80,96},{96,112},{112,0},{1... | collective-permute-start | bytes 331784 | tf_op jit(solution)/shard_map/ppermute | solution.py:20
  550.2 7.9 %collective-permute-start.21 = (bf16[18,6,1,512]{3,1,0,2:T(8,128)(2,1)}, bf16[18,6,1,512]{3,1,0,2:T(8,128)(2,1)S(1)}, u32[]{:S(2)}, u32[]{:S(2)}) collective-permute-start(bf16[18,6,1,512]{3,1,0,2:T(8,128)(2,1)} %get-tuple-element.171), channel_id=1, source_target_pairs={{16,0},{32,16},{48,32},{64,48},{80,64},{96,80},{112,96},{0,112},{1... | collective-permute-start | bytes 331784 | tf_op jit(solution)/shard_map/ppermute | solution.py:21
  562.7 20.3 %copy-start.12 = (f32[12,24,1,512]{3,2,1,0:T(1,128)S(1)}, f32[12,24,1,512]{3,2,1,0:T(1,128)}, u32[]{:S(2)}) copy-start(f32[12,24,1,512]{3,2,1,0:T(1,128)} %param.45) | copy-start | bytes 1769476
  562.7 20.3 %copy-start.59 = (f32[12,24]{1,0:T(8,128)S(1)}, f32[12,24]{1,0:T(8,128)}, u32[]{:S(2)}) copy-start(f32[12,24]{1,0:T(8,128)} %copy-done.58) | copy-start | bytes 3460
  562.7 20.3 %copy-start.105 = (f32[512]{0:T(512)S(1)}, f32[512]{0:T(512)}, u32[]{:S(2)}) copy-start(f32[512]{0:T(512)} %param.47) | copy-start | bytes 6148
  563.9 19.2 %copy-start.47 = (bf16[288,512]{1,0:T(8,128)(2,1)S(1)}, bf16[288,512]{1,0:T(8,128)(2,1)}, u32[]{:S(2)}) copy-start(bf16[288,512]{1,0:T(8,128)(2,1)} %convolution_convert_fusion.21) | copy-start | bytes 884740
  566.6 16.7 %copy-start.85 = (f32[12,24]{1,0:T(8,128)S(1)}, f32[12,24]{1,0:T(8,128)}, u32[]{:S(2)}) copy-start(f32[12,24]{1,0:T(8,128)} %copy-done.84) | copy-start | bytes 3460
  566.6 16.7 %copy-start.72 = (f32[12,24]{1,0:T(8,128)S(1)}, f32[12,24]{1,0:T(8,128)}, u32[]{:S(2)}) copy-start(f32[12,24]{1,0:T(8,128)} %copy-done.71) | copy-start | bytes 3460
  568.7 8.1 %collective-permute-start.22 = (bf16[3,24,1,512]{3,1,0,2:T(8,128)(2,1)S(1)}, bf16[3,24,1,512]{3,1,0,2:T(8,128)(2,1)S(1)}, u32[]{:S(2)}, u32[]{:S(2)}) collective-permute-start(bf16[3,24,1,512]{3,1,0,2:T(8,128)(2,1)S(1)} %get-tuple-element.180), channel_id=1, source_target_pairs={{0,1},{1,2},{2,3},{3,4},{4,5},{5,6},{6,7},{7,8},{8,9},{9,10},{10,1... | collective-permute-start | bytes 221192 | tf_op jit(solution)/shard_map/ppermute | solution.py:20
  574.9 7.2 %collective-permute-start.23 = (bf16[3,24,1,512]{3,1,0,2:T(8,128)(2,1)S(1)}, bf16[3,24,1,512]{3,1,0,2:T(8,128)(2,1)S(1)}, u32[]{:S(2)}, u32[]{:S(2)}) collective-permute-start(bf16[3,24,1,512]{3,1,0,2:T(8,128)(2,1)S(1)} %get-tuple-element.181), channel_id=1, source_target_pairs={{1,0},{2,1},{3,2},{4,3},{5,4},{6,5},{7,6},{8,7},{9,8},{10,9},{11,1... | collective-permute-start | bytes 221192 | tf_op jit(solution)/shard_map/ppermute | solution.py:21
  (95 other events, 468.5 us)
where the time goes:
time: 597 us; the launch traced here: 586 us
  local copies, waits for them, and re-layouts  286 us (48%)
  matrix products  101 us (17%)
  other arithmetic  96.9 us (16%)
  starting transfers between devices  73.2 us (12%)
  waiting for transfers between devices  25.3 us (4%)
    convert_element_type x21, local copies, waits for them, and re-layouts, unit_heads(): tensor.astype(jnp.float32)  64.1 us
    dot_general x22, matrix products, project(): result = jnp.dot(flattened, weight, preferred_element_type=jnp.float32)  53.2 us
    ppermute x12, starting transfers between devices, with_halo(): before = lax.ppermute(last, axis, up)  40.1 us
    ppermute x12, starting transfers between devices, with_halo(): after = lax.ppermute(leading, axis, down)  33.1 us
    dot_general x9, matrix products, attend(): jnp.einsum('abqhd,abkhd->abhqk', queries, keys, preferred_element_type=jn...  27.2 us
    convert_element_type x9, other arithmetic, unit_heads(): tensor.astype(jnp.float32)  21.7 us
    reshape x8, local copies, waits for them, and re-layouts, to_windows(): tensor.reshape(extent // WLAT, WLAT, across // WLON, WLON, levels, channels)  20.9 us
    dot_general x9, matrix products, attend(): jnp.einsum('abhqk,abkhd->abqhd', probs, values, preferred_element_type=jn...  20.9 us
  transfers between devices with their start and end apart: 24, of which 8 were waited for; matrix products, arithmetic and copies ran while one was open for 14% of the time, Pallas kernels for 0%

commit v1 on v0

v1 whole, which is shorter than its diff:
```python
import functools

import jax
import jax.numpy as jnp
import numpy as np
from jax import lax
from jax.experimental import pallas as pl
from jax.experimental.pallas import tpu as pltpu
from jax.sharding import PartitionSpec as P

WLAT = 6
WLON = 12
EPS = 1e-05
ROWS, COLS = 12, 24
HOME = ROWS * COLS
PAD = 80
BODY = 4 * PAD
CELLS = WLAT * WLON
PIECES = ((0, 64), (64, 64), (128, 32))
SENT = 160
D = 512
DC = 1024
F32 = jnp.float32
BF16 = jnp.bfloat16


def fine_order(r, c):
    return PAD * (2 * (r // WLAT) + c // WLON) + (r % WLAT) * WLON + c % WLON


def plane_order(r, c):
    return PAD * (2 * (r % 2) + c % 2) + (r // 2) * WLON + c // 2


def home_order(r, c):
    return r * COLS + c


def piece_row(r, c):
    if r >= 9 and c < 18:
        return (r - 9) * 18 + c
    if r < 9 and c >= 18:
        return 64 + r * 6 + (c - 18)
    if r >= 9 and c >= 18:
        return 128 + (r - 9) * 6 + (c - 18)
    return None


def move_matrices(order_a, rows_a, order_b, rows_b):
    pick = np.zeros((SENT, rows_a), np.float32)
    own = np.zeros((rows_b, rows_a), np.float32)
    place = np.zeros((rows_b, SENT), np.float32)
    for r in range(ROWS):
        for c in range(COLS):
            piece = piece_row(r, c)
            if piece is not None:
                pick[piece, order_a(r, c)] = 1
            ra, ca = (r - 3) % ROWS, (c - 6) % COLS
            if r >= 3 and c >= 6:
                own[order_b(r, c), order_a(ra, ca)] = 1
            else:
                place[order_b(r, c), piece_row(ra, ca)] = 1
    return pick, own, place


def all_moves():
    first = move_matrices(home_order, HOME, fine_order, BODY)
    second = move_matrices(fine_order, BODY, plane_order, BODY)
    pick, own, place = first
    moves = [pick, own, place, place.T, own.T, pick.T]
    pick, own, place = second
    moves += [pick, own, place, place.T, own.T, pick.T]
    return [np.ascontiguousarray(m).astype(jnp.bfloat16) for m in moves]


def mm(a, b):
    return lax.dot_general(a, b, (((1,), (0,)), ((), ())), preferred_element_type=F32)


def mm_nt(a, b):
    return lax.dot_general(a, b, (((1,), (1,)), ((), ())), preferred_element_type=F32)


def mm_tn(a, b):
    return lax.dot_general(a, b, (((0,), (0,)), ((), ())), preferred_element_type=F32)


def row_mean(x):
    return jnp.mean(x, axis=-1, keepdims=True)


def at_rows(g, n=PAD):
    if isinstance(g, int):
        return pl.ds(g * n, n)
    return pl.ds(pl.multiple_of(g * n, n), n)


def at_lanes(j, n):
    if isinstance(j, int):
        return pl.ds(j * n, n)
    return pl.ds(pl.multiple_of(j * n, n), n)


def head_sums():
    shape = (256, 256)
    a = lax.broadcasted_iota(jnp.int32, shape, 0) // 64
    b = lax.broadcasted_iota(jnp.int32, shape, 1) // 64
    return jnp.where(a == b, 1.0, 0.0).astype(BF16)


def pair_masks():
    lane = lax.broadcasted_iota(jnp.int32, (PAD, 128), 1)
    return lane < 64


def stack_pair(x, low):
    zero = jnp.zeros_like(x)
    return jnp.concatenate([jnp.where(low, x, zero), jnp.where(low, zero, x)], axis=0)


class Block:
    def __init__(self, rows, channels, gain, wq, wkv, wo, scale, kept, sums):
        self.rows, self.channels = rows, channels
        self.gain, self.wq, self.wkv, self.wo, self.scale = gain, wq, wkv, wo, scale
        self.xhat, self.rstd, self.uq, self.uk, self.rq, self.rk, self.v, self.probs = kept
        self.sums = sums
        self.groups = rows // PAD * (channels // 512)

    def tile(self, g):
        if self.channels == 512:
            return at_rows(g), 0, 0
        return at_rows(0), g, 8 * g

    def norm_rows(self, g, x, n_ref):
        centred = x - row_mean(x)
        rstd = lax.rsqrt(row_mean(centred * centred) + EPS)
        xhat = centred * rstd
        self.xhat[at_rows(g), :] = xhat
        self.rstd[at_rows(g), :] = jnp.broadcast_to(rstd, (PAD, 128))
        n_ref[at_rows(g), :] = (xhat * self.gain[...]).astype(BF16)

    def project(self, n_ref):
        channels = self.channels

        def unit(weight, at, u_ref, r_ref):
            raw = mm(n_ref[...], weight[:, at]).astype(BF16).astype(F32)
            r = lax.rsqrt(mm((raw * raw).astype(BF16), self.sums[...]) + 1.0)
            r_ref[:, at] = r
            u_ref[:, at] = (raw * r).astype(BF16)

        def body(j, carry):
            at = at_lanes(j, 256)
            unit(self.wq, at, self.uq, self.rq)
            unit(self.wkv, at, self.uk, self.rk)
            behind = at_lanes(j + channels // 256, 256)
            self.v[:, at] = mm(n_ref[...], self.wkv[:, behind]).astype(BF16)
            return carry

        lax.fori_loop(0, channels // 256, body, 0)

    def scales(self, head):
        top = lax.broadcasted_iota(jnp.int32, (2 * PAD, 1), 0) < PAD
        return jnp.where(top, self.scale[head], self.scale[head + 1])

    def attend(self, mask_ref, mixed_ref):
        low = pair_masks()

        def body(g, carry):
            rows, block, head0 = self.tile(g)
            if self.channels == 512:
                mask = mask_ref[g // 2]
            else:
                mask = mask_ref[0]
            for p in range(4):
                lanes = at_lanes(4 * block + p, 128)
                queries = stack_pair(self.uq[rows, lanes], low)
                scores = mm_nt(queries, self.uk[rows, lanes])
                weights = jnp.exp(scores * self.scales(head0 + 2 * p)) * mask
                total = jnp.sum(weights, axis=-1, keepdims=True)
                probs = (weights * (1.0 / total)).astype(BF16)
                self.probs[4 * g + p] = probs
                both = mm(probs, self.v[rows, lanes])
                mixed_ref[rows, lanes] = jnp.where(low, both[:PAD], both[PAD:]).astype(BF16)
            return carry

        lax.fori_loop(0, self.groups, body, 0)

    def outward(self, mixed_ref, add):
        def body(j, carry):
            at = at_lanes(j, 256)
            add(at, mm(mixed_ref[...], self.wo[:, at]))
            return carry

        lax.fori_loop(0, self.channels // 256, body, 0)

    def backward(self, grad_ref, dmixed_ref, duq_ref, duk_ref, dqkv_ref, dn_ref):
        channels = self.channels
        low = pair_masks()

        def out_body(j, carry):
            at = at_lanes(j, 256)
            dmixed_ref[:, at] = mm_nt(grad_ref[...], self.wo[at, :]).astype(BF16)
            return carry

        lax.fori_loop(0, channels // 256, out_body, 0)

        def body(g, carry):
            rows, block, head0 = self.tile(g)
            for p in range(4):
                lanes = at_lanes(4 * block + p, 128)
                behind = at_lanes(4 * block + p + 2 * (channels // 128), 128)
                douts = stack_pair(dmixed_ref[rows, lanes], low)
                keys = self.uk[rows, lanes]
                queries = stack_pair(self.uq[rows, lanes], low)
                probs = self.probs[4 * g + p]
                dprobs = mm_nt(douts, self.v[rows, lanes])
                wide = probs.astype(F32)
                weighed = wide * dprobs
                total = jnp.sum(weighed, axis=-1, keepdims=True)
                scale = self.scales(head0 + 2 * p)
                dscores = ((weighed - wide * total) * scale).astype(BF16)
                dqkv_ref[rows, behind] = mm_tn(probs, douts).astype(BF16)
                both = mm(dscores, keys)
                duq_ref[rows, lanes] = jnp.where(low, both[:PAD], both[PAD:])
                duk_ref[rows, lanes] = mm_tn(dscores, queries)
            return carry

        lax.fori_loop(0, self.groups, body, 0)

        def unit_body(j, carry):
            at = at_lanes(j, 256)
            shifted = at_lanes(j + channels // 256, 256)
            for u_ref, r_ref, du_ref, to in (
                (self.uq, self.rq, duq_ref, at),
                (self.uk, self.rk, duk_ref, shifted),
            ):
                u = u_ref[:, at].astype(F32)
                du = du_ref[:, at]
                inner = mm((u * du).astype(BF16), self.sums[...])
                dqkv_ref[:, to] = (r_ref[:, at] * (du - u * inner)).astype(BF16)
            return carry

        lax.fori_loop(0, channels // 256, unit_body, 0)

        def in_body(j, carry):
            at = at_lanes(j, 256)
            dn_ref[:, at] = mm_nt(dqkv_ref[:, :channels], self.wq[at, :]) + mm_nt(
                dqkv_ref[:, channels:], self.wkv[at, :]
            )
            return carry

        lax.fori_loop(0, channels // 256, in_body, 0)

    def norm_backward(self, g, dn):
        dy = dn * self.gain[...]
        xhat = self.xhat[at_rows(g), :]
        rstd = self.rstd[at_rows(g), :][:, :1]
        return rstd * (dy - row_mean(dy) - xhat * row_mean(dy * xhat))


WEIGHTS = (
    "encoder_query",
    "encoder_keyval",
    "encoder_output",
    "merge_weight",
    "coarse_query",
    "coarse_keyval",
    "coarse_output",
    "expand_weight",
    "decoder_query",
    "decoder_keyval",
    "decoder_output",
)


def kept_shapes(rows, channels):
    units = rows // PAD * (channels // 128)
    return [
        ((rows, channels), F32),
        ((rows, 128), F32),
        ((rows, channels), BF16),
        ((rows, channels), BF16),
        ((rows, channels), F32),
        ((rows, channels), F32),
        ((rows, channels), BF16),
        ((units, 2 * PAD, PAD), BF16),
    ]


def scratch_table():
    table = {}
    for block, rows, channels in (("enc", BODY, D), ("dec", BODY, D), ("crs", PAD, DC)):
        table[block] = kept_shapes(rows, channels)
    for kind, rows, channels in (("fine", BODY, D), ("coarse", PAD, DC)):
        table[kind] = [
            ((rows, channels), BF16),
            ((rows, channels), BF16),
            ((rows, channels), F32),
            ((rows, channels), F32),
            ((rows, 3 * channels), BF16),
            ((rows, channels), F32),
            ((rows, channels), F32),
            ((rows, channels), BF16),
        ]
    table["misc"] = [
        ((HOME, D), BF16),
        ((HOME, D), BF16),
        ((BODY, D), F32),
        ((BODY, D), F32),
        ((BODY, D), F32),
        ((PAD, 4 * D), F32),
        ((PAD, 128), F32),
        ((PAD, 4 * D), BF16),
        ((PAD, DC), F32),
        ((PAD, 128), F32),
        ((PAD, 4 * D), BF16),
        ((HOME, D), F32),
        ((2, 2 * PAD, PAD), F32),
        ((256, 256), BF16),
        ((8, SENT, D), BF16),
        ((8, SENT, D), BF16),
    ]
    return table


TABLE = scratch_table()
NAMES = tuple(TABLE)


def kernel(*refs):
    refs = list(refs)

    def take(n):
        head = refs[:n]
        del refs[:n]
        return head

    fields_in, cot_in = take(2)
    weights_in = take(len(WEIGHTS))
    moves_in = take(12)
    enc_gain, merge_gain, crs_gain, exp_gain, dec_gain = take(5)
    enc_scale, crs_scale, dec_scale = take(3)
    out_ref, grad_ref = take(2)
    fields_v, cot_v = take(2)
    weights = take(len(WEIGHTS))
    moves = take(12)
    spaces = {name: take(len(TABLE[name])) for name in NAMES}
    local_sem, send_sem, recv_sem = take(3)

    lat, lon = lax.axis_index("lat"), lax.axis_index("lon")
    nlat, nlon = lax.axis_size("lat"), lax.axis_size("lon")

    loads = []
    order = [(fields_in, fields_v), (moves_in[0], moves[0]), (moves_in[1], moves[1])]
    order += [(moves_in[2], moves[2]), (cot_in, cot_v)]
    order += list(zip(weights_in[:3], weights[:3]))
    order += list(zip(moves_in[6:9], moves[6:9]))
    order += list(zip(weights_in[3:8], weights[3:8]))
    order += list(zip(moves_in[9:], moves[9:]))
    order += list(zip(weights_in[8:], weights[8:]))
    order += list(zip(moves_in[3:6], moves[3:6]))
    for k, (src, dst) in enumerate(order):
        copy = pltpu.make_async_copy(src, dst, local_sem.at[k])
        copy.start()
        loads.append(copy)
    waited = [0]

    def loaded(upto):
        while waited[0] < upto:
            loads[waited[0]].wait()
            waited[0] += 1

    def device(dlat, dlon):
        return {
            "lat": lax.rem(lat + dlat + nlat, nlat),
            "lon": lax.rem(lon + dlon + nlon, nlon),
        }

    onward = (device(1, 0), device(0, 1), device(1, 1))
    back = (device(-1, 0), device(0, -1), device(-1, -1))
    barrier = pltpu.get_barrier_semaphore()
    for target in onward + back:
        pl.semaphore_signal(
            barrier, inc=1, device_id=target, device_id_type=pl.DeviceIdType.MESH
        )

    (
        fields_b,
        cot_b,
        cot_f,
        gskip,
        planes,
        m_xhat,
        m_rstd,
        merged,
        e_xhat,
        e_rstd,
        dexp,
        home,
        mask_ref,
        sums,
        sent,
        received,
    ) = spaces["misc"]

    shape = (2 * PAD, PAD)
    q = lax.broadcasted_iota(jnp.int32, shape, 0)
    q = jnp.where(q >= PAD, q - PAD, q)
    k = lax.broadcasted_iota(jnp.int32, shape, 1)
    there = jnp.where(k < CELLS, 1, 0)
    apart = jnp.where((q < CELLS // 2) == (k < CELLS // 2), 0, 1)
    first = jnp.where(lat == 0, 1, 0)
    mask_ref[0] = (there * (1 - apart * first)).astype(F32)
    mask_ref[1] = there.astype(F32)
    sums[...] = head_sums()

    started = []

    def send(t, source, pick, targets):
        sent[t] = mm(pick[...], source[...]).astype(BF16)
        for n, (start, size) in enumerate(PIECES):
            copy = pltpu.make_async_remote_copy(
                src_ref=sent.at[t, pl.ds(start, size)],
                dst_ref=received.at[t, pl.ds(start, size)],
                send_sem=send_sem.at[t, n],
                recv_sem=recv_sem.at[t, n],
                device_id=targets[n],
                device_id_type=pl.DeviceIdType.MESH,
            )
            copy.start()
            started.append(copy)

    def arrive(t):
        for copy in started[3 * t : 3 * t + 3]:
            copy.wait_recv()

    def rows_loop(body, count=4):
        def step(g, carry):
            body(g)
            return carry

        lax.fori_loop(0, count, step, 0)

    def flat(ref, to):
        for n in range(4):
            part = ref[pl.ds(n, HOME, stride=4), :]
            to[:, pl.ds(128 * n, 128)] = part.astype(BF16)

    def unflat(ref, frm):
        for n in range(4):
            ref[pl.ds(n, HOME, stride=4), :] = frm[:, 128 * n : 128 * (n + 1)]

    encoder = Block(
        BODY, D, enc_gain, weights[0], weights[1], weights[2], enc_scale, spaces["enc"], sums
    )
    coarse = Block(
        PAD, DC, crs_gain, weights[4], weights[5], weights[6], crs_scale, spaces["crs"], sums
    )
    decoder = Block(
        BODY, D, dec_gain, weights[8], weights[9], weights[10], dec_scale, spaces["dec"], sums
    )
    merge_w, expand_w = weights[3], weights[7]
    fn, fmixed, fduq, fduk, fdqkv, fdn, fx, fb = spaces["fine"]
    cn, cmixed, cduq, cduk, cdqkv, cdn, cx, cb = spaces["coarse"]

    loaded(2)
    flat(fields_v, fields_b)
    pl.semaphore_wait(barrier, 6)
    send(0, fields_b, moves[0], onward)
    loaded(5)
    flat(cot_v, cot_b)
    send(1, cot_b, moves[0], onward)

    def own_fields(g):
        fx[at_rows(g), :] = mm(moves[1][at_rows(g), :], fields_b[...])
        cot_f[at_rows(g), :] = mm(moves[1][at_rows(g), :], cot_b[...])

    rows_loop(own_fields)
    loaded(11)
    arrive(0)

    def enter_encoder(g):
        x = fx[at_rows(g), :] + mm(moves[2][at_rows(g), :], received[0])
        fx[at_rows(g), :] = x
        encoder.norm_rows(g, x, fn)

    rows_loop(enter_encoder)
    encoder.project(fn)
    encoder.attend(mask_ref, fmixed)

    def add_encoder(at, branch):
        x = fx[:, at] + branch
        fx[:, at] = x
        fb[:, at] = x.astype(BF16)

    encoder.outward(fmixed, add_encoder)

    send(2, fb, moves[6], onward)

    def own_section(g):
        planes[at_rows(g), :] = mm(moves[7][at_rows(g), :], fb[...])

    rows_loop(own_section)
    loaded(len(loads))
    arrive(2)
    total = jnp.zeros((PAD, D), F32)
    for p in range(4):
        x = planes[at_rows(p), :] + mm(moves[8][at_rows(p), :], received[2])
        planes[at_rows(p), :] = x
        total += x
    mean = jnp.sum(total, axis=-1, keepdims=True) * (1.0 / (4 * D))
    total = jnp.zeros((PAD, D), F32)
    for p in range(4):
        centred = planes[at_rows(p), :] - mean
        total += centred * centred
    rstd = lax.rsqrt(jnp.sum(total, axis=-1, keepdims=True) * (1.0 / (4 * D)) + EPS)
    m_rstd[...] = jnp.broadcast_to(rstd, (PAD, 128))
    for p in range(4):
        lanes = at_lanes(p, D)
        xhat = (planes[at_rows(p), :] - mean) * rstd
        m_xhat[:, lanes] = xhat
        merged[:, lanes] = (xhat * merge_gain[:, lanes]).astype(BF16)

    def merge_body(j):
        at = at_lanes(j, 256)
        cx[:, at] = mm(merged[...], merge_w[:, at])

    rows_loop(merge_body)
    coarse.norm_rows(0, cx[...], cn)
    coarse.project(cn)
    coarse.attend(mask_ref, cmixed)

    def add_coarse(at, branch):
        cx[:, at] = cx[:, at] + branch

    coarse.outward(cmixed, add_coarse)

    x = cx[...]
    centred = x - row_mean(x)
    rstd = lax.rsqrt(row_mean(centred * centred) + EPS)
    xhat = centred * rstd
    e_xhat[...] = xhat
    e_rstd[...] = jnp.broadcast_to(rstd, (PAD, 128))
    cb[...] = (xhat * exp_gain[...]).astype(BF16)

    def expand_body(p):
        fb[at_rows(p), :] = mm(cb[...], expand_w[:, at_lanes(p, D)]).astype(BF16)

    rows_loop(expand_body)

    send(3, fb, moves[9], back)

    def own_expanded(g):
        fx[at_rows(g), :] = fx[at_rows(g), :] + mm(moves[10][at_rows(g), :], fb[...])

    rows_loop(own_expanded)
    arrive(3)

    def enter_decoder(g):
        x = fx[at_rows(g), :] + mm(moves[11][at_rows(g), :], received[3])
        fx[at_rows(g), :] = x
        decoder.norm_rows(g, x, fn)

    rows_loop(enter_decoder)
    decoder.project(fn)
    decoder.attend(mask_ref, fmixed)

    def add_decoder(at, branch):
        fb[:, at] = (fx[:, at] + branch).astype(BF16)

    decoder.outward(fmixed, add_decoder)

    send(4, fb, moves[3], back)
    home[...] = mm(moves[4][...], fb[...])

    arrive(1)

    def enter_gradient(g):
        x = cot_f[at_rows(g), :] + mm(moves[2][at_rows(g), :], received[1])
        cot_f[at_rows(g), :] = x
        fb[at_rows(g), :] = x.astype(BF16)

    rows_loop(enter_gradient)
    decoder.backward(fb, fn, fduq, fduk, fdqkv, fdn)

    def leave_decoder(g):
        x = cot_f[at_rows(g), :] + decoder.norm_backward(g, fdn[at_rows(g), :])
        gskip[at_rows(g), :] = x
        fb[at_rows(g), :] = x.astype(BF16)

    rows_loop(leave_decoder)

    send(5, fb, moves[6], onward)
    rows_loop(own_section)
    arrive(4)
    unflat(out_ref, home[...] + mm(moves[5][...], received[4]))
    arrive(5)
    for p in range(4):
        x = planes[at_rows(p), :] + mm(moves[8][at_rows(p), :], received[5])
        dexp[:, at_lanes(p, D)] = x.astype(BF16)

    def expand_back(j):
        at = at_lanes(j, 256)
        cdn[:, at] = mm_nt(dexp[...], expand_w[at, :])

    rows_loop(expand_back)
    dy = cdn[...] * exp_gain[...]
    xhat = e_xhat[...]
    x = e_rstd[:, :1] * (dy - row_mean(dy) - xhat * row_mean(dy * xhat))
    cx[...] = x
    cb[...] = x.astype(BF16)
    coarse.backward(cb, cn, cduq, cduk, cdqkv, cdn)
    cb[...] = (cx[...] + coarse.norm_backward(0, cdn[...])).astype(BF16)

    def merge_back(p):
        planes[at_rows(p), :] = mm_nt(cb[...], merge_w[at_rows(p, D), :])

    rows_loop(merge_back)
    total = jnp.zeros((PAD, D), F32)
    weighed = jnp.zeros((PAD, D), F32)
    for p in range(4):
        lanes = at_lanes(p, D)
        dy = planes[at_rows(p), :] * merge_gain[:, lanes]
        total += dy
        weighed += dy * m_xhat[:, lanes]
    mean = jnp.sum(total, axis=-1, keepdims=True) * (1.0 / (4 * D))
    tilt = jnp.sum(weighed, axis=-1, keepdims=True) * (1.0 / (4 * D))
    rstd = m_rstd[:, :1]
    for p in range(4):
        lanes = at_lanes(p, D)
        dy = planes[at_rows(p), :] * merge_gain[:, lanes]
        fb[at_rows(p), :] = (rstd * (dy - mean - m_xhat[:, lanes] * tilt)).astype(BF16)

    send(6, fb, moves[9], back)

    def own_gradient(g):
        gskip[at_rows(g), :] = gskip[at_rows(g), :] + mm(moves[10][at_rows(g), :], fb[...])

    rows_loop(own_gradient)
    arrive(6)

    def enter_encoder_gradient(g):
        x = gskip[at_rows(g), :] + mm(moves[11][at_rows(g), :], received[6])
        gskip[at_rows(g), :] = x
        fb[at_rows(g), :] = x.astype(BF16)

    rows_loop(enter_encoder_gradient)
    encoder.backward(fb, fn, fduq, fduk, fdqkv, fdn)

    def leave_encoder(g):
        x = gskip[at_rows(g), :] + encoder.norm_backward(g, fdn[at_rows(g), :])
        fb[at_rows(g), :] = x.astype(BF16)

    rows_loop(leave_encoder)

    send(7, fb, moves[3], back)
    home[...] = mm(moves[4][...], fb[...])
    arrive(7)
    unflat(grad_ref, home[...] + mm(moves[5][...], received[7]))
    for copy in started:
        copy.wait_send()


def shards(
    fields,
    cotangent,
    encoder_gain,
    encoder_query,
    encoder_keyval,
    encoder_output,
    encoder_scale,
    merge_gain,
    merge_weight,
    coarse_gain,
    coarse_query,
    coarse_keyval,
    coarse_output,
    coarse_scale,
    expand_gain,
    expand_weight,
    decoder_gain,
    decoder_query,
    decoder_keyval,
    decoder_output,
    decoder_scale,
):
    shape = fields.shape
    weights = (
        encoder_query,
        encoder_keyval,
        encoder_output,
        merge_weight,
        coarse_query,
        coarse_keyval,
        coarse_output,
        expand_weight,
        decoder_query,
        decoder_keyval,
        decoder_output,
    )
    moves = [jnp.asarray(m) for m in all_moves()]
    gains = [
        g.reshape(1, -1)
        for g in (encoder_gain, merge_gain, coarse_gain, expand_gain, decoder_gain)
    ]
    scales = (encoder_scale, coarse_scale, decoder_scale)
    flat = (HOME * 4, 128)
    anywhere = pl.BlockSpec(memory_space=pl.ANY)
    in_vmem = pl.BlockSpec(memory_space=pltpu.VMEM)
    in_smem = pl.BlockSpec(memory_space=pltpu.SMEM)
    scratch = [pltpu.VMEM(flat, F32)] * 2
    scratch += [pltpu.VMEM(w.shape, BF16) for w in weights]
    scratch += [pltpu.VMEM(m.shape, BF16) for m in moves]
    for name in NAMES:
        scratch += [pltpu.VMEM(s, t) for s, t in TABLE[name]]
    scratch += [
        pltpu.SemaphoreType.DMA((2 + len(weights) + len(moves),)),
        pltpu.SemaphoreType.DMA((8, 3)),
        pltpu.SemaphoreType.DMA((8, 3)),
    ]
    output, grad = pl.pallas_call(
        kernel,
        out_shape=(jax.ShapeDtypeStruct(flat, F32),) * 2,
        in_specs=[anywhere] * (2 + len(weights) + len(moves)) + [in_vmem] * 5 + [in_smem] * 3,
        out_specs=(in_vmem, in_vmem),
        scratch_shapes=scratch,
        compiler_params=pltpu.CompilerParams(
            collective_id=0, has_side_effects=True, vmem_limit_bytes=60 * 1024 * 1024
        ),
    )(
        fields.reshape(flat),
        cotangent.reshape(flat),
        *weights,
        *moves,
        *gains,
        *scales,
    )
    return (output.reshape(shape), grad.reshape(shape))


def solution(mesh):
    along = P("lat", "lon", None, None)
    return jax.shard_map(
        shards,
        mesh=mesh,
        in_specs=(along, along) + (P(),) * 19,
        out_specs=(along, along),
        check_vma=False,
    )
```

time: 597 us -> 94.1 us (0.16)
  the two profiles are of different devices: /device:TPU:1 before, /device:TPU:0 now
where the time goes in v1:
time: 94.1 us; the launch traced here: 93.8 us
  Pallas kernels  88.6 us (94%)
  local copies, waits for them, and re-layouts  4.57 us (5%)
    pallas_call x1, Pallas kernels, shards(): pl.pallas_call(kernel, out_shape=(jax.ShapeDtypeStruct(flat, F32),) * 2,...  88.6 us
    unnamed x2, local copies, waits for them, and re-layouts  4.57 us

profile of v1, /device:TPU:0, one launch (start us, length us, event | category | flops | bytes accessed | tf_op | source)
XLA Modules:
  0.0 93.8 jit_solution(8663199546639376077)
XLA Ops:
  0.6 88.6 %shard_map.320 = (f32[1152,128]{1,0:T(8,128)}, f32[1152,128]{1,0:T(8,128)}) custom-call(f32[1152,128]{1,0:T(8,128)} %bitcast.9, f32[1152,128]{1,0:T(8,128)} %bitcast.10, bf16[512,512]{1,0:T(8,128)(2,1)} %refs_2_.1, bf16[512,1024]{1,0:T(8,128)(2,1)} %refs_3_.1, bf16[512,512]{1,0:T(8,128)(2,1)} %refs_4_.1, bf16[2048,1024]{1,0:T(8,128)(2,1)} %refs_5_.1, ...), custom_call_target="tpu_custom_call" | custom-call | tf_op jit(solution)/shard_map/pallas_call | solution.py:721
  89.2 2.3 %copy.39 = f32[12,24,1,512]{3,2,1,0:T(1,128)} copy(f32[12,24,1,512]{3,2,1,0:T(1,128)} %bitcast.12) | data formatting | bytes 1179648
  91.5 2.3 %copy.40 = f32[12,24,1,512]{3,2,1,0:T(1,128)} copy(f32[12,24,1,512]{3,2,1,0:T(1,128)} %bitcast.11) | data formatting | bytes 1179648

commit v2 on v1

v2 whole, which is shorter than its diff:
```python
import functools

import jax
import jax.numpy as jnp
import numpy as np
from jax import lax
from jax.experimental import pallas as pl
from jax.experimental.pallas import tpu as pltpu
from jax.sharding import PartitionSpec as P

WLAT = 6
WLON = 12
EPS = 1e-05
ROWS, COLS = 12, 24
HOME = ROWS * COLS
PAD = 80
BODY = 4 * PAD
CELLS = WLAT * WLON
PIECES = ((0, 64), (64, 64), (128, 32))
SENT = 160
D = 512
DC = 1024
F32 = jnp.float32
BF16 = jnp.bfloat16
LOG2E = 1.4426950408889634


def fine_order(r, c):
    return PAD * (2 * (r // WLAT) + c // WLON) + (r % WLAT) * WLON + c % WLON


def plane_order(r, c):
    return PAD * (2 * (r % 2) + c % 2) + (r // 2) * WLON + c // 2


def home_order(r, c):
    return r * COLS + c


def piece_row(r, c):
    if r >= 9 and c < 18:
        return (r - 9) * 18 + c
    if r < 9 and c >= 18:
        return 64 + r * 6 + (c - 18)
    if r >= 9 and c >= 18:
        return 128 + (r - 9) * 6 + (c - 18)
    return None


def move_matrices(order_a, rows_a, order_b, rows_b):
    pick = np.zeros((SENT, rows_a), np.float32)
    own = np.zeros((rows_b, rows_a), np.float32)
    place = np.zeros((rows_b, SENT), np.float32)
    for r in range(ROWS):
        for c in range(COLS):
            piece = piece_row(r, c)
            if piece is not None:
                pick[piece, order_a(r, c)] = 1
            ra, ca = (r - 3) % ROWS, (c - 6) % COLS
            if r >= 3 and c >= 6:
                own[order_b(r, c), order_a(ra, ca)] = 1
            else:
                place[order_b(r, c), piece_row(ra, ca)] = 1
    return pick, own, place


def all_moves():
    first = move_matrices(home_order, HOME, fine_order, BODY)
    second = move_matrices(fine_order, BODY, plane_order, BODY)
    pick, own, place = first
    moves = [pick, own, place, place.T, own.T, pick.T]
    pick, own, place = second
    moves += [pick, own, place, place.T, own.T, pick.T]
    return [np.ascontiguousarray(m).astype(jnp.bfloat16) for m in moves]


def mm(a, b):
    return lax.dot_general(a, b, (((1,), (0,)), ((), ())), preferred_element_type=F32)


def mm_nt(a, b):
    return lax.dot_general(a, b, (((1,), (1,)), ((), ())), preferred_element_type=F32)


def mm_tn(a, b):
    return lax.dot_general(a, b, (((0,), (0,)), ((), ())), preferred_element_type=F32)


def row_mean(x):
    return jnp.mean(x, axis=-1, keepdims=True)


def at_rows(g, n=PAD):
    if isinstance(g, int):
        return pl.ds(g * n, n)
    return pl.ds(pl.multiple_of(g * n, n), n)


def at_lanes(j, n):
    if isinstance(j, int):
        return pl.ds(j * n, n)
    return pl.ds(pl.multiple_of(j * n, n), n)


def head_sums():
    shape = (256, 256)
    a = lax.broadcasted_iota(jnp.int32, shape, 0) // 64
    b = lax.broadcasted_iota(jnp.int32, shape, 1) // 64
    return jnp.where(a == b, 1.0, 0.0).astype(BF16)


def pair_masks():
    lane = lax.broadcasted_iota(jnp.int32, (PAD, 128), 1)
    return lane < 64


def stack_pair(x, low):
    zero = jnp.zeros_like(x)
    return jnp.concatenate([jnp.where(low, x, zero), jnp.where(low, zero, x)], axis=0)


def pick_pair(x, low):
    return jnp.where(low, x[:PAD], x[PAD:])


def beside(a, b):
    return jnp.concatenate([a, b], axis=1)


def bar_queries(first):
    shape = (2 * PAD, 128)
    q = lax.broadcasted_iota(jnp.int32, shape, 0)
    q = jnp.where(q >= PAD, q - PAD, q)
    lane = lax.broadcasted_iota(jnp.int32, shape, 1)
    upper = jnp.where(q < CELLS // 2, first, 0)
    lower = jnp.where(q < CELLS // 2, 0, first)
    value = jnp.where(lane == 0, upper, jnp.where(lane == 1, lower, 0))
    return jnp.where(lane == 2, 1, value).astype(F32).astype(BF16)


def bar_keys():
    shape = (PAD, 128)
    k = lax.broadcasted_iota(jnp.int32, shape, 0)
    lane = lax.broadcasted_iota(jnp.int32, shape, 1)
    upper = jnp.where(k < CELLS // 2, 1, 0)
    there = jnp.where(k < CELLS, 1, 0)
    value = jnp.where(lane == 0, there - upper, jnp.where(lane == 1, upper, 0))
    value = jnp.where(lane == 2, 1 - there, value)
    return (value * -1024).astype(F32).astype(BF16)


class Block:
    def __init__(self, rows, channels, gain, wq, wkv, wo, scale, kept, sums):
        self.rows, self.channels = rows, channels
        self.gain, self.wq, self.wkv, self.wo, self.scale = gain, wq, wkv, wo, scale
        self.xhat, self.rstd, self.uq, self.uk, self.rq, self.rk = kept[:6]
        self.v, self.weights, self.inverse, self.mixed = kept[6:]
        self.sums = sums
        pairs = channels // 128
        self.units = [(g, p) for g in range(rows // PAD) for p in range(pairs)]

    def chunks(self):
        return [pl.ds(at, 512) for at in range(0, self.channels, 512)]

    def tiles(self, ref):
        return [ref[at_rows(g), at_lanes(p, 128)] for g, p in self.units]

    def norm_rows(self, g, x, n_ref):
        centred = x - row_mean(x)
        rstd = lax.rsqrt(row_mean(centred * centred) + EPS)
        xhat = centred * rstd
        self.xhat[at_rows(g), :] = xhat
        self.rstd[at_rows(g), :] = jnp.broadcast_to(rstd, (PAD, 128))
        n_ref[at_rows(g), :] = (xhat * self.gain[...]).astype(BF16)

    def head_total(self, x):
        sums = self.sums[...]
        return beside(mm(x[:, :256], sums), mm(x[:, 256:], sums))

    def project(self, n_ref):
        def unit(weight, at, u_ref, r_ref):
            raw = mm(n_ref[...], weight[:, at]).astype(BF16).astype(F32)
            r = lax.rsqrt(self.head_total((raw * raw).astype(BF16)) + 1.0)
            r_ref[:, at] = r
            u_ref[:, at] = (raw * r).astype(BF16)

        for at in self.chunks():
            unit(self.wq, at, self.uq, self.rq)
            unit(self.wkv, at, self.uk, self.rk)
            behind = pl.ds(at.start + self.channels, 512)
            self.v[:, at] = mm(n_ref[...], self.wkv[:, behind]).astype(BF16)

    def scales(self, p, factor):
        top = lax.broadcasted_iota(jnp.int32, (2 * PAD, 1), 0) < PAD
        return jnp.where(top, self.scale[2 * p] * factor, self.scale[2 * p + 1] * factor)

    def attend(self, barred, bar_key):
        low = pair_masks()
        ones = jnp.ones((PAD, 128), BF16)
        queries = [stack_pair(q, low) for q in self.tiles(self.uq)]
        keys, values = self.tiles(self.uk), self.tiles(self.v)
        scores = [
            mm_nt(beside(q, barred(g)), beside(k, bar_key))
            for q, k, (g, p) in zip(queries, keys, self.units)
        ]
        weights = [
            jnp.exp2(s * self.scales(p, LOG2E)).astype(BF16)
            for s, (g, p) in zip(scores, self.units)
        ]
        both = [mm(w, beside(v, ones)) for w, v in zip(weights, values)]
        for n, (g, p) in enumerate(self.units):
            at = (at_rows(g), at_lanes(p, 128))
            self.weights[n] = weights[n]
            inverse = 1.0 / pick_pair(both[n][:, 128:], low)
            self.inverse[at] = inverse
            self.mixed[at] = (pick_pair(both[n][:, :128], low) * inverse).astype(BF16)

    def mixed_back(self, grad_ref, dmixed_ref):
        for at in self.chunks():
            dmixed_ref[:, at] = mm_nt(grad_ref[...], self.wo[at, :]).astype(BF16)

    def attend_back(self, dmixed_ref, duq_ref, duk_ref, dqkv_ref):
        low = pair_masks()
        ones = jnp.ones((PAD, 128), BF16)
        divided = [
            d.astype(F32) * i for d, i in zip(self.tiles(dmixed_ref), self.tiles(self.inverse))
        ]
        shift = [
            stack_pair((-(d * m.astype(F32))).astype(BF16), low)
            for d, m in zip(divided, self.tiles(self.mixed))
        ]
        douts = [stack_pair(d.astype(BF16), low) for d in divided]
        queries = [stack_pair(q, low) for q in self.tiles(self.uq)]
        keys, values = self.tiles(self.uk), self.tiles(self.v)
        weights = [self.weights[n] for n in range(len(self.units))]
        dprobs = [
            mm_nt(beside(d, s), beside(v, ones)) for d, s, v in zip(douts, shift, values)
        ]
        dscores = [
            (w.astype(F32) * (d * self.scales(p, 1.0))).astype(BF16)
            for w, d, (g, p) in zip(weights, dprobs, self.units)
        ]
        dvalues = [mm_tn(w, d) for w, d in zip(weights, douts)]
        dkeys = [mm_tn(d, q) for d, q in zip(dscores, queries)]
        dqueries = [mm(d, k) for d, k in zip(dscores, keys)]
        for n, (g, p) in enumerate(self.units):
            at = (at_rows(g), at_lanes(p, 128))
            behind = at_lanes(p + 2 * (self.channels // 128), 128)
            dqkv_ref[at_rows(g), behind] = dvalues[n].astype(BF16)
            duk_ref[at] = dkeys[n].astype(BF16)
            duq_ref[at] = pick_pair(dqueries[n], low).astype(BF16)

    def project_back(self, duq_ref, duk_ref, dqkv_ref, dn_ref):
        channels = self.channels
        for at in self.chunks():
            shifted = pl.ds(at.start + channels, 512)
            for u_ref, r_ref, du_ref, to in (
                (self.uq, self.rq, duq_ref, at),
                (self.uk, self.rk, duk_ref, shifted),
            ):
                u = u_ref[:, at].astype(F32)
                du = du_ref[:, at].astype(F32)
                inner = self.head_total((u * du).astype(BF16))
                dqkv_ref[:, to] = (r_ref[:, at] * (du - u * inner)).astype(BF16)
        for at in self.chunks():
            dn_ref[:, at] = mm_nt(dqkv_ref[:, :channels], self.wq[at, :]) + mm_nt(
                dqkv_ref[:, channels:], self.wkv[at, :]
            )

    def norm_backward(self, g, dn):
        dy = dn * self.gain[...]
        xhat = self.xhat[at_rows(g), :]
        rstd = self.rstd[at_rows(g), :][:, :1]
        return rstd * (dy - row_mean(dy) - xhat * row_mean(dy * xhat))


WEIGHTS = (
    "encoder_query",
    "encoder_keyval",
    "encoder_output",
    "merge_weight",
    "coarse_query",
    "coarse_keyval",
    "coarse_output",
    "expand_weight",
    "decoder_query",
    "decoder_keyval",
    "decoder_output",
)


def kept_shapes(rows, channels):
    units = rows // PAD * (channels // 128)
    return [
        ((rows, channels), F32),
        ((rows, 128), F32),
        ((rows, channels), BF16),
        ((rows, channels), BF16),
        ((rows, channels), F32),
        ((rows, channels), F32),
        ((rows, channels), BF16),
        ((units, 2 * PAD, PAD), BF16),
        ((rows, channels), F32),
        ((rows, channels), BF16),
    ]


def scratch_table():
    table = {}
    for block, rows, channels in (("enc", BODY, D), ("dec", BODY, D), ("crs", PAD, DC)):
        table[block] = kept_shapes(rows, channels)
    for kind, rows, channels in (("fine", BODY, D), ("coarse", PAD, DC)):
        table[kind] = [
            ((rows, channels), BF16),
            ((rows, channels), BF16),
            ((rows, channels), BF16),
            ((rows, channels), BF16),
            ((rows, 3 * channels), BF16),
            ((rows, channels), F32),
            ((rows, channels), F32),
            ((rows, channels), BF16),
        ]
    table["misc"] = [
        ((HOME, D), BF16),
        ((HOME, D), BF16),
        ((HOME, D), BF16),
        ((HOME, D), BF16),
        ((BODY, D), F32),
        ((BODY, D), F32),
        ((BODY, D), F32),
        ((PAD, 4 * D), F32),
        ((PAD, 128), F32),
        ((PAD, 4 * D), BF16),
        ((PAD, DC), F32),
        ((PAD, 128), F32),
        ((PAD, 4 * D), BF16),
        ((BODY, D), BF16),
        ((HOME, D), F32),
        ((HOME, D), F32),
        ((HOME * 4, 128), F32),
        ((HOME * 4, 128), BF16),
        ((HOME * 4, 128), BF16),
        ((2, 2 * PAD, 128), BF16),
        ((PAD, 128), BF16),
        ((256, 256), BF16),
        ((8, SENT, D), BF16),
        ((8, SENT, D), BF16),
    ]
    return table


TABLE = scratch_table()
NAMES = tuple(TABLE)


def kernel(*refs):
    refs = list(refs)

    def take(n):
        head = refs[:n]
        del refs[:n]
        return head

    fields_in, cot_in = take(2)
    weights_in = take(len(WEIGHTS))
    moves_in = take(12)
    enc_gain, merge_gain, crs_gain, exp_gain, dec_gain = take(5)
    enc_scale, crs_scale, dec_scale = take(3)
    out_hbm, grad_hbm = take(2)
    fields_v, cot_v = take(2)
    weights = take(len(WEIGHTS))
    moves = take(12)
    spaces = {name: take(len(TABLE[name])) for name in NAMES}
    local_sem, out_sem, send_sem, recv_sem = take(4)

    lat, lon = lax.axis_index("lat"), lax.axis_index("lon")
    nlat, nlon = lax.axis_size("lat"), lax.axis_size("lon")

    loads = []
    waited = [0]

    def load(*pairs):
        for src, dst in pairs:
            copy = pltpu.make_async_copy(src, dst, local_sem.at[len(loads)])
            copy.start()
            loads.append(copy)

    def loaded(upto):
        while waited[0] < upto:
            loads[waited[0]].wait()
            waited[0] += 1

    def weight(*which):
        return [(weights_in[n], weights[n]) for n in which]

    def move(*which):
        return [(moves_in[n], moves[n]) for n in which]

    load((fields_in, fields_v), *move(0))

    def device(dlat, dlon):
        return {
            "lat": lax.rem(lat + dlat + nlat, nlat),
            "lon": lax.rem(lon + dlon + nlon, nlon),
        }

    onward = (device(1, 0), device(0, 1), device(1, 1))
    back = (device(-1, 0), device(0, -1), device(-1, -1))
    barrier = pltpu.get_barrier_semaphore()
    for target in onward + back:
        pl.semaphore_signal(
            barrier, inc=1, device_id=target, device_id_type=pl.DeviceIdType.MESH
        )

    (
        fields_b,
        fields_rest,
        cot_b,
        cot_rest,
        cot_f,
        gskip,
        planes,
        m_xhat,
        m_rstd,
        merged,
        e_xhat,
        e_rstd,
        dexp,
        out_b,
        out_home,
        grad_home,
        by_cell,
        out_cells,
        grad_cells,
        bar_q,
        bar_k,
        sums,
        sent,
        received,
    ) = spaces["misc"]

    bar_q[0] = bar_queries(jnp.where(lat == 0, 1, 0))
    bar_q[1] = bar_queries(0)
    bar_k[...] = bar_keys()
    sums[...] = head_sums()

    started = {}

    def prepare(t, source, pick):
        sent[t] = mm(pick[...], source[...]).astype(BF16)

    def launch(t, targets):
        started[t] = []
        for n, (start, size) in enumerate(PIECES):
            copy = pltpu.make_async_remote_copy(
                src_ref=sent.at[t, pl.ds(start, size)],
                dst_ref=received.at[t, pl.ds(start, size)],
                send_sem=send_sem.at[t, n],
                recv_sem=recv_sem.at[t, n],
                device_id=targets[n],
                device_id_type=pl.DeviceIdType.MESH,
            )
            copy.start()
            started[t].append(copy)

    def arrive(t):
        for copy in started[t]:
            copy.wait_recv()

    def by_rows(body):
        for g in range(4):
            body(g, at_rows(g))

    def flat(ref, to, rest):
        for n in range(4):
            part = ref[pl.ds(n, HOME, stride=4), :]
            rounded = part.astype(BF16)
            to[:, at_lanes(n, 128)] = rounded
            rest[:, at_lanes(n, 128)] = (part - rounded.astype(F32)).astype(BF16)

    outs = []

    def deliver(x, cells, ref):
        for n in range(4):
            by_cell[pl.ds(n, HOME, stride=4), :] = x[:, 128 * n : 128 * (n + 1)]
        cells[...] = by_cell[...].astype(BF16)
        copy = pltpu.make_async_copy(cells, ref, out_sem.at[len(outs)])
        copy.start()
        outs.append(copy)

    encoder = Block(
        BODY, D, enc_gain, weights[0], weights[1], weights[2], enc_scale, spaces["enc"], sums
    )
    coarse = Block(
        PAD, DC, crs_gain, weights[4], weights[5], weights[6], crs_scale, spaces["crs"], sums
    )
    decoder = Block(
        BODY, D, dec_gain, weights[8], weights[9], weights[10], dec_scale, spaces["dec"], sums
    )
    merge_w, expand_w = weights[3], weights[7]
    fn, fdmixed, fduq, fduk, fdqkv, fdn, fx, fb = spaces["fine"]
    cn, cdmixed, cduq, cduk, cdqkv, cdn, cx, cb = spaces["coarse"]

    def fine_bar(g):
        return bar_q[g // 2]

    def coarse_bar(g):
        return bar_q[0]

    loaded(2)
    flat(fields_v, fields_b, fields_rest)
    prepare(0, fields_b, moves[0])
    pl.semaphore_wait(barrier, 6)
    launch(0, onward)
    load(*move(1), (cot_in, cot_v), *move(2), *weight(0, 1, 2))
    loaded(4)
    fx[...] = mm(moves[1][...], fields_b[...]) + mm(moves[1][...], fields_rest[...])
    flat(cot_v, cot_b, cot_rest)
    prepare(1, cot_b, moves[0])
    cot_f[...] = mm(moves[1][...], cot_b[...]) + mm(moves[1][...], cot_rest[...])
    loaded(8)
    arrive(0)
    launch(1, onward)
    load(*move(6, 7, 8), *weight(3, 4, 5, 6, 7), *move(9, 10, 11), *weight(8, 9, 10))
    load(*move(3, 4, 5))

    def enter_encoder(g, at):
        x = fx[at, :] + mm(moves[2][at, :], received[0])
        fx[at, :] = x
        encoder.norm_rows(g, x, fn)

    by_rows(enter_encoder)
    encoder.project(fn)
    encoder.attend(fine_bar, bar_k[...])
    section = fx[...] + mm(encoder.mixed[...], encoder.wo[...])
    fx[...] = section
    fb[...] = section.astype(BF16)

    loaded(11)
    prepare(2, fb, moves[6])
    launch(2, onward)
    planes[...] = mm(moves[7][...], fb[...])
    arrive(1)
    cot = cot_f[...] + mm(moves[2][...], received[1])
    cot_f[...] = cot
    out_b[...] = cot.astype(BF16)
    loaded(len(loads))
    decoder.mixed_back(out_b, fdmixed)
    arrive(2)
    total = jnp.zeros((PAD, D), F32)
    for p in range(4):
        x = planes[at_rows(p), :] + mm(moves[8][at_rows(p), :], received[2])
        planes[at_rows(p), :] = x
        total += x
    mean = jnp.sum(total, axis=-1, keepdims=True) * (1.0 / (4 * D))
    total = jnp.zeros((PAD, D), F32)
    for p in range(4):
        centred = planes[at_rows(p), :] - mean
        total += centred * centred
    rstd = lax.rsqrt(jnp.sum(total, axis=-1, keepdims=True) * (1.0 / (4 * D)) + EPS)
    m_rstd[...] = jnp.broadcast_to(rstd, (PAD, 128))
    for p in range(4):
        lanes = at_lanes(p, D)
        xhat = (planes[at_rows(p), :] - mean) * rstd
        m_xhat[:, lanes] = xhat
        merged[:, lanes] = (xhat * merge_gain[:, lanes]).astype(BF16)
    cx[...] = mm(merged[...], merge_w[...])
    coarse.norm_rows(0, cx[...], cn)
    coarse.project(cn)
    coarse.attend(coarse_bar, bar_k[...])
    x = cx[...] + mm(coarse.mixed[...], coarse.wo[...])
    centred = x - row_mean(x)
    rstd = lax.rsqrt(row_mean(centred * centred) + EPS)
    xhat = centred * rstd
    e_xhat[...] = xhat
    e_rstd[...] = jnp.broadcast_to(rstd, (PAD, 128))
    cb[...] = (xhat * exp_gain[...]).astype(BF16)
    for p in range(4):
        fb[at_rows(p), :] = mm(cb[...], expand_w[:, at_lanes(p, D)]).astype(BF16)

    prepare(3, fb, moves[9])
    launch(3, back)
    fx[...] = fx[...] + mm(moves[10][...], fb[...])
    arrive(3)

    def enter_decoder(g, at):
        x = fx[at, :] + mm(moves[11][at, :], received[3])
        fx[at, :] = x
        decoder.norm_rows(g, x, fn)

    by_rows(enter_decoder)
    decoder.project(fn)
    decoder.attend(fine_bar, bar_k[...])
    out_b[...] = (fx[...] + mm(decoder.mixed[...], decoder.wo[...])).astype(BF16)

    decoder.attend_back(fdmixed, fduq, fduk, fdqkv)
    decoder.project_back(fduq, fduk, fdqkv, fdn)

    def leave_decoder(g, at):
        x = cot_f[at, :] + decoder.norm_backward(g, fdn[at, :])
        gskip[at, :] = x
        fb[at, :] = x.astype(BF16)

    by_rows(leave_decoder)

    prepare(5, fb, moves[6])
    launch(5, onward)
    planes[...] = mm(moves[7][...], fb[...])
    prepare(4, out_b, moves[3])
    out_home[...] = mm(moves[4][...], out_b[...])
    arrive(5)
    launch(4, back)
    for p in range(4):
        x = planes[at_rows(p), :] + mm(moves[8][at_rows(p), :], received[5])
        dexp[:, at_lanes(p, D)] = x.astype(BF16)
    dy = mm_nt(dexp[...], expand_w[...]) * exp_gain[...]
    xhat = e_xhat[...]
    x = e_rstd[:, :1] * (dy - row_mean(dy) - xhat * row_mean(dy * xhat))
    cx[...] = x
    cb[...] = x.astype(BF16)
    coarse.mixed_back(cb, cdmixed)
    coarse.attend_back(cdmixed, cduq, cduk, cdqkv)
    coarse.project_back(cduq, cduk, cdqkv, cdn)
    cb[...] = (cx[...] + coarse.norm_backward(0, cdn[...])).astype(BF16)
    for p in range(4):
        planes[at_rows(p), :] = mm_nt(cb[...], merge_w[at_rows(p, D), :])
    total = jnp.zeros((PAD, D), F32)
    weighed = jnp.zeros((PAD, D), F32)
    for p in range(4):
        lanes = at_lanes(p, D)
        dy = planes[at_rows(p), :] * merge_gain[:, lanes]
        total += dy
        weighed += dy * m_xhat[:, lanes]
    mean = jnp.sum(total, axis=-1, keepdims=True) * (1.0 / (4 * D))
    tilt = jnp.sum(weighed, axis=-1, keepdims=True) * (1.0 / (4 * D))
    rstd = m_rstd[:, :1]
    for p in range(4):
        lanes = at_lanes(p, D)
        dy = planes[at_rows(p), :] * merge_gain[:, lanes]
        fb[at_rows(p), :] = (rstd * (dy - mean - m_xhat[:, lanes] * tilt)).astype(BF16)

    prepare(6, fb, moves[9])
    launch(6, back)
    gskip[...] = gskip[...] + mm(moves[10][...], fb[...])
    arrive(4)
    deliver(out_home[...] + mm(moves[5][...], received[4]), out_cells, out_hbm)
    arrive(6)
    x = gskip[...] + mm(moves[11][...], received[6])
    gskip[...] = x
    fb[...] = x.astype(BF16)
    encoder.mixed_back(fb, fdmixed)
    encoder.attend_back(fdmixed, fduq, fduk, fdqkv)
    encoder.project_back(fduq, fduk, fdqkv, fdn)

    def leave_encoder(g, at):
        x = gskip[at, :] + encoder.norm_backward(g, fdn[at, :])
        fb[at, :] = x.astype(BF16)

    by_rows(leave_encoder)

    prepare(7, fb, moves[3])
    launch(7, back)
    grad_home[...] = mm(moves[4][...], fb[...])
    arrive(7)
    deliver(grad_home[...] + mm(moves[5][...], received[7]), grad_cells, grad_hbm)
    for t in started:
        for copy in started[t]:
            copy.wait_send()
    for copy in outs:
        copy.wait()


def shards(
    fields,
    cotangent,
    encoder_gain,
    encoder_query,
    encoder_keyval,
    encoder_output,
    encoder_scale,
    merge_gain,
    merge_weight,
    coarse_gain,
    coarse_query,
    coarse_keyval,
    coarse_output,
    coarse_scale,
    expand_gain,
    expand_weight,
    decoder_gain,
    decoder_query,
    decoder_keyval,
    decoder_output,
    decoder_scale,
):
    shape = fields.shape
    weights = (
        encoder_query,
        encoder_keyval,
        encoder_output,
        merge_weight,
        coarse_query,
        coarse_keyval,
        coarse_output,
        expand_weight,
        decoder_query,
        decoder_keyval,
        decoder_output,
    )
    moves = [jnp.asarray(m) for m in all_moves()]
    gains = [
        g.reshape(1, -1)
        for g in (encoder_gain, merge_gain, coarse_gain, expand_gain, decoder_gain)
    ]
    scales = (encoder_scale, coarse_scale, decoder_scale)
    flat = (HOME * 4, 128)
    anywhere = pl.BlockSpec(memory_space=pl.ANY)
    in_vmem = pl.BlockSpec(memory_space=pltpu.VMEM)
    in_smem = pl.BlockSpec(memory_space=pltpu.SMEM)
    scratch = [pltpu.VMEM(flat, F32)] * 2
    scratch += [pltpu.VMEM(w.shape, BF16) for w in weights]
    scratch += [pltpu.VMEM(m.shape, BF16) for m in moves]
    for name in NAMES:
        scratch += [pltpu.VMEM(s, t) for s, t in TABLE[name]]
    scratch += [
        pltpu.SemaphoreType.DMA((2 + len(weights) + len(moves),)),
        pltpu.SemaphoreType.DMA((2,)),
        pltpu.SemaphoreType.DMA((8, 3)),
        pltpu.SemaphoreType.DMA((8, 3)),
    ]
    output, grad = pl.pallas_call(
        kernel,
        out_shape=(jax.ShapeDtypeStruct(flat, BF16),) * 2,
        in_specs=[anywhere] * (2 + len(weights) + len(moves)) + [in_vmem] * 5 + [in_smem] * 3,
        out_specs=(anywhere, anywhere),
        scratch_shapes=scratch,
        compiler_params=pltpu.CompilerParams(
            collective_id=0, has_side_effects=True, vmem_limit_bytes=60 * 1024 * 1024
        ),
    )(
        fields.reshape(flat),
        cotangent.reshape(flat),
        *weights,
        *moves,
        *gains,
        *scales,
    )
    return (output.astype(F32).reshape(shape), grad.astype(F32).reshape(shape))


def solution(mesh):
    along = P("lat", "lon", None, None)
    return jax.shard_map(
        shards,
        mesh=mesh,
        in_specs=(along, along) + (P(),) * 19,
        out_specs=(along, along),
        check_vma=False,
    )
```

time: 94.1 us -> 63.9 us (0.68)
  the two profiles are of different devices: /device:TPU:0 before, /device:TPU:1 now
where the time goes in v2:
time: 63.9 us; the launch traced here: 62.8 us
  Pallas kernels  58.5 us (92%)
  other arithmetic  3.63 us (6%)
  between operations  0.65 us (1%)
    pallas_call x1, Pallas kernels, shards(): pl.pallas_call(kernel, out_shape=(jax.ShapeDtypeStruct(flat, BF16),) * 2,...  58.5 us
    reshape x2, other arithmetic, shards(): return (output.astype(F32).reshape(shape), grad.astype(F32).reshape(shape))  3.63 us

profile of v2, /device:TPU:1, one launch (start us, length us, event | category | flops | bytes accessed | tf_op | source)
XLA Modules:
  0.0 62.8 jit_solution(4346859036704261246)
XLA Ops:
  0.6 58.5 %shard_map.320 = (bf16[1152,128]{1,0:T(8,128)(2,1)}, bf16[1152,128]{1,0:T(8,128)(2,1)}) custom-call(f32[1152,128]{1,0:T(8,128)} %bitcast.9, f32[1152,128]{1,0:T(8,128)} %bitcast.10, bf16[512,512]{1,0:T(8,128)(2,1)} %refs_2_.1, bf16[512,1024]{1,0:T(8,128)(2,1)} %refs_3_.1, bf16[512,512]{1,0:T(8,128)(2,1)} %refs_4_.1, bf16[2048,1024]{1,0:T(8,128)(2,1)} %refs_5_.1, ...), custom_call_target="tpu_custom_call" | custom-call | tf_op jit(solution)/shard_map/pallas_call | solution.py:731
  59.1 1.8 %reshape.48 = f32[1152,128]{1,0:T(8,128)} convert(bf16[1152,128]{1,0:T(8,128)(2,1)} %get-tuple-element.4) | non-fusion elementwise | flops 147456 | bytes 884736 | tf_op jit(solution)/shard_map/reshape | solution.py:748
  60.9 1.8 %reshape.50 = f32[1152,128]{1,0:T(8,128)} convert(bf16[1152,128]{1,0:T(8,128)(2,1)} %get-tuple-element.5) | non-fusion elementwise | flops 147456 | bytes 884736 | tf_op jit(solution)/shard_map/reshape | solution.py:748

commit v3 on v2

--- a/solution.py
+++ b/solution.py
@@ -68,9 +68,9 @@
     first = move_matrices(home_order, HOME, fine_order, BODY)
     second = move_matrices(fine_order, BODY, plane_order, BODY)
     pick, own, place = first
-    moves = [pick, own, place, place.T, own.T, pick.T]
+    moves = [pick, own, place, place.T[:, : 3 * PAD], own.T, pick.T]
     pick, own, place = second
-    moves += [pick, own, place, place.T, own.T, pick.T]
+    moves += [pick[:, PAD:], own, place, place.T, own.T, pick.T]
     return [np.ascontiguousarray(m).astype(jnp.bfloat16) for m in moves]
 
 
@@ -156,14 +156,20 @@
         self.xhat, self.rstd, self.uq, self.uk, self.rq, self.rk = kept[:6]
         self.v, self.weights, self.inverse, self.mixed = kept[6:]
         self.sums = sums
-        pairs = channels // 128
-        self.units = [(g, p) for g in range(rows // PAD) for p in range(pairs)]
+        self.pairs = channels // 128
+        self.every = range(rows // PAD)
 
     def chunks(self):
         return [pl.ds(at, 512) for at in range(0, self.channels, 512)]
 
-    def tiles(self, ref):
-        return [ref[at_rows(g), at_lanes(p, 128)] for g, p in self.units]
+    def rows_of(self, windows):
+        return pl.ds(PAD * windows.start, PAD * len(windows))
+
+    def units(self, windows):
+        return [(g, p) for g in windows for p in range(self.pairs)]
+
+    def tiles(self, ref, units):
+        return [ref[at_rows(g), at_lanes(p, 128)] for g, p in units]
 
     def norm_rows(self, g, x, n_ref):
         centred = x - row_mean(x)
@@ -177,94 +183,104 @@
         sums = self.sums[...]
         return beside(mm(x[:, :256], sums), mm(x[:, 256:], sums))
 
-    def project(self, n_ref):
+    def project(self, windows, n_ref):
+        rows = self.rows_of(windows)
+
         def unit(weight, at, u_ref, r_ref):
-            raw = mm(n_ref[...], weight[:, at]).astype(BF16).astype(F32)
+            raw = mm(n_ref[rows, :], weight[:, at]).astype(BF16).astype(F32)
             r = lax.rsqrt(self.head_total((raw * raw).astype(BF16)) + 1.0)
-            r_ref[:, at] = r
-            u_ref[:, at] = (raw * r).astype(BF16)
+            r_ref[rows, at] = r
+            u_ref[rows, at] = (raw * r).astype(BF16)
 
         for at in self.chunks():
             unit(self.wq, at, self.uq, self.rq)
             unit(self.wkv, at, self.uk, self.rk)
             behind = pl.ds(at.start + self.channels, 512)
-            self.v[:, at] = mm(n_ref[...], self.wkv[:, behind]).astype(BF16)
+            self.v[rows, at] = mm(n_ref[rows, :], self.wkv[:, behind]).astype(BF16)
 
     def scales(self, p, factor):
         top = lax.broadcasted_iota(jnp.int32, (2 * PAD, 1), 0) < PAD
         return jnp.where(top, self.scale[2 * p] * factor, self.scale[2 * p + 1] * factor)
 
-    def attend(self, barred, bar_key):
+    def attend(self, windows, barred, bar_key):
         low = pair_masks()
         ones = jnp.ones((PAD, 128), BF16)
-        queries = [stack_pair(q, low) for q in self.tiles(self.uq)]
-        keys, values = self.tiles(self.uk), self.tiles(self.v)
+        units = self.units(windows)
+        queries = [stack_pair(q, low) for q in self.tiles(self.uq, units)]
+        keys, values = self.tiles(self.uk, units), self.tiles(self.v, units)
         scores = [
             mm_nt(beside(q, barred(g)), beside(k, bar_key))
-            for q, k, (g, p) in zip(queries, keys, self.units)
+            for q, k, (g, p) in zip(queries, keys, units)
         ]
         weights = [
             jnp.exp2(s * self.scales(p, LOG2E)).astype(BF16)
-            for s, (g, p) in zip(scores, self.units)
+            for s, (g, p) in zip(scores, units)
         ]
         both = [mm(w, beside(v, ones)) for w, v in zip(weights, values)]
-        for n, (g, p) in enumerate(self.units):
+        for n, (g, p) in enumerate(units):
             at = (at_rows(g), at_lanes(p, 128))
-            self.weights[n] = weights[n]
+            self.weights[self.pairs * g + p] = weights[n]
             inverse = 1.0 / pick_pair(both[n][:, 128:], low)
             self.inverse[at] = inverse
             self.mixed[at] = (pick_pair(both[n][:, :128], low) * inverse).astype(BF16)
 
-    def mixed_back(self, grad_ref, dmixed_ref):
+    def branch(self, windows):
+        return mm(self.mixed[self.rows_of(windows), :], self.wo[...])
+
+    def mixed_back(self, windows, grad_ref, dmixed_ref):
+        rows = self.rows_of(windows)
         for at in self.chunks():
-            dmixed_ref[:, at] = mm_nt(grad_ref[...], self.wo[at, :]).astype(BF16)
-
-    def attend_back(self, dmixed_ref, duq_ref, duk_ref, dqkv_ref):
+            dmixed_ref[rows, at] = mm_nt(grad_ref[rows, :], self.wo[at, :]).astype(BF16)
+
+    def attend_back(self, windows, dmixed_ref, duq_ref, duk_ref, dqkv_ref):
         low = pair_masks()
         ones = jnp.ones((PAD, 128), BF16)
+        units = self.units(windows)
         divided = [
-            d.astype(F32) * i for d, i in zip(self.tiles(dmixed_ref), self.tiles(self.inverse))
+            d.astype(F32) * i
+            for d, i in zip(self.tiles(dmixed_ref, units), self.tiles(self.inverse, units))
         ]
         shift = [
             stack_pair((-(d * m.astype(F32))).astype(BF16), low)
-            for d, m in zip(divided, self.tiles(self.mixed))
+            for d, m in zip(divided, self.tiles(self.mixed, units))
         ]
         douts = [stack_pair(d.astype(BF16), low) for d in divided]
-        queries = [stack_pair(q, low) for q in self.tiles(self.uq)]
-        keys, values = self.tiles(self.uk), self.tiles(self.v)
-        weights = [self.weights[n] for n in range(len(self.units))]
+        queries = [stack_pair(q, low) for q in self.tiles(self.uq, units)]
+        keys, values = self.tiles(self.uk, units), self.tiles(self.v, units)
+        weights = [self.weights[self.pairs * g + p] for g, p in units]
         dprobs = [
             mm_nt(beside(d, s), beside(v, ones)) for d, s, v in zip(douts, shift, values)
         ]
         dscores = [
             (w.astype(F32) * (d * self.scales(p, 1.0))).astype(BF16)
-            for w, d, (g, p) in zip(weights, dprobs, self.units)
+            for w, d, (g, p) in zip(weights, dprobs, units)
         ]
         dvalues = [mm_tn(w, d) for w, d in zip(weights, douts)]
         dkeys = [mm_tn(d, q) for d, q in zip(dscores, queries)]
         dqueries = [mm(d, k) for d, k in zip(dscores, keys)]
-        for n, (g, p) in enumerate(self.units):
+        for n, (g, p) in enumerate(units):
             at = (at_rows(g), at_lanes(p, 128))
-            behind = at_lanes(p + 2 * (self.channels // 128), 128)
+            behind = at_lanes(p + 2 * self.pairs, 128)
             dqkv_ref[at_rows(g), behind] = dvalues[n].astype(BF16)
             duk_ref[at] = dkeys[n].astype(BF16)
             duq_ref[at] = pick_pair(dqueries[n], low).astype(BF16)
 
-    def project_back(self, duq_ref, duk_ref, dqkv_ref, dn_ref):
+    def project_back(self, windows, duq_ref, duk_ref, dqkv_ref, dn_ref):
         channels = self.channels
+        rows = self.rows_of(windows)
         for at in self.chunks():
             shifted = pl.ds(at.start + channels, 512)
             for u_ref, r_ref, du_ref, to in (
                 (self.uq, self.rq, duq_ref, at),
                 (self.uk, self.rk, duk_ref, shifted),
             ):
-                u = u_ref[:, at].astype(F32)
-                du = du_ref[:, at].astype(F32)
+                u = u_ref[rows, at].astype(F32)
+                du = du_ref[rows, at].astype(F32)
                 inner = self.head_total((u * du).astype(BF16))
-                dqkv_ref[:, to] = (r_ref[:, at] * (du - u * inner)).astype(BF16)
+                dqkv_ref[rows, to] = (r_ref[rows, at] * (du - u * inner)).astype(BF16)
         for at in self.chunks():
-            dn_ref[:, at] = mm_nt(dqkv_ref[:, :channels], self.wq[at, :]) + mm_nt(
-                dqkv_ref[:, channels:], self.wkv[at, :]
+            dn_ref[rows, at] = mm_nt(dqkv_ref[rows, :channels], self.wq[at, :]) + mm_nt(
+                dqkv_ref[rows, channels:], self.wkv[at, :]
             )
 
     def norm_backward(self, g, dn):
@@ -338,8 +354,7 @@
         ((HOME, D), F32),
         ((HOME, D), F32),
         ((HOME * 4, 128), F32),
-        ((HOME * 4, 128), BF16),
-        ((HOME * 4, 128), BF16),
+        ((2, HOME * 4, 128), BF16),
         ((2, 2 * PAD, 128), BF16),
         ((PAD, 128), BF16),
         ((256, 256), BF16),
@@ -366,7 +381,7 @@
     moves_in = take(12)
     enc_gain, merge_gain, crs_gain, exp_gain, dec_gain = take(5)
     enc_scale, crs_scale, dec_scale = take(3)
-    out_hbm, grad_hbm = take(2)
+    (out_hbm,) = take(1)
     fields_v, cot_v = take(2)
     weights = take(len(WEIGHTS))
     moves = take(12)
@@ -396,7 +411,7 @@
     def move(*which):
         return [(moves_in[n], moves[n]) for n in which]
 
-    load((fields_in, fields_v), *move(0))
+    load((fields_in, fields_v), *move(0, 1), (cot_in, cot_v), *weight(0, 1, 2))
 
     def device(dlat, dlon):
         return {
@@ -431,7 +446,6 @@
         grad_home,
         by_cell,
         out_cells,
-        grad_cells,
         bar_q,
         bar_k,
         sums,
@@ -447,7 +461,7 @@
     started = {}
 
     def prepare(t, source, pick):
-        sent[t] = mm(pick[...], source[...]).astype(BF16)
+        sent[t] = mm(pick[...], source).astype(BF16)
 
     def launch(t, targets):
         started[t] = []
@@ -467,10 +481,6 @@
         for copy in started[t]:
             copy.wait_recv()
 
-    def by_rows(body):
-        for g in range(4):
-            body(g, at_rows(g))
-
     def flat(ref, to, rest):
         for n in range(4):
             part = ref[pl.ds(n, HOME, stride=4), :]
@@ -480,11 +490,11 @@
 
     outs = []
 
-    def deliver(x, cells, ref):
+    def deliver(x, which):
         for n in range(4):
             by_cell[pl.ds(n, HOME, stride=4), :] = x[:, 128 * n : 128 * (n + 1)]
-        cells[...] = by_cell[...].astype(BF16)
-        copy = pltpu.make_async_copy(cells, ref, out_sem.at[len(outs)])
+        out_cells[which] = by_cell[...].astype(BF16)
+        copy = pltpu.make_async_copy(out_cells.at[which], out_hbm.at[which], out_sem.at[which])
         copy.start()
         outs.append(copy)
 
@@ -507,45 +517,73 @@
     def coarse_bar(g):
         return bar_q[0]
 
+    def encode(windows):
+        rows = encoder.rows_of(windows)
+        encoder.project(windows, fn)
+        encoder.attend(windows, fine_bar, bar_k[...])
+        section = fx[rows, :] + encoder.branch(windows)
+        fx[rows, :] = section
+        fb[rows, :] = section.astype(BF16)
+
+    def decode(windows):
+        rows = decoder.rows_of(windows)
+        for g in windows:
+            decoder.norm_rows(g, fx[at_rows(g), :], fn)
+        decoder.project(windows, fn)
+        decoder.attend(windows, fine_bar, bar_k[...])
+        out_b[rows, :] = (fx[rows, :] + decoder.branch(windows)).astype(BF16)
+        decoder.attend_back(windows, fdmixed, fduq, fduk, fdqkv)
+        decoder.project_back(windows, fduq, fduk, fdqkv, fdn)
+        for g in windows:
+            at = at_rows(g)
+            x = cot_f[at, :] + decoder.norm_backward(g, fdn[at, :])
+            gskip[at, :] = x
+            fb[at, :] = x.astype(BF16)
+
+    def encode_back(windows):
+        encoder.mixed_back(windows, fb, fdmixed)
+        encoder.attend_back(windows, fdmixed, fduq, fduk, fdqkv)
+        encoder.project_back(windows, fduq, fduk, fdqkv, fdn)
+        for g in windows:
+            at = at_rows(g)
+            x = gskip[at, :] + encoder.norm_backward(g, fdn[at, :])
+            fb[at, :] = x.astype(BF16)
+
     loaded(2)
     flat(fields_v, fields_b, fields_rest)
-    prepare(0, fields_b, moves[0])
+    prepare(0, fields_b[...], moves[0])
     pl.semaphore_wait(barrier, 6)
     launch(0, onward)
-    load(*move(1), (cot_in, cot_v), *move(2), *weight(0, 1, 2))
+    load(*move(2, 6, 7, 8), *weight(3, 4, 5, 6, 7), *move(9, 10, 11), *weight(8, 9, 10))
+    load(*move(3, 4, 5))
     loaded(4)
     fx[...] = mm(moves[1][...], fields_b[...]) + mm(moves[1][...], fields_rest[...])
     flat(cot_v, cot_b, cot_rest)
-    prepare(1, cot_b, moves[0])
+    prepare(1, cot_b[...], moves[0])
     cot_f[...] = mm(moves[1][...], cot_b[...]) + mm(moves[1][...], cot_rest[...])
+    loaded(7)
+    encoder.norm_rows(3, fx[at_rows(3), :], fn)
+    encode(range(3, 4))
     loaded(8)
     arrive(0)
     launch(1, onward)
-    load(*move(6, 7, 8), *weight(3, 4, 5, 6, 7), *move(9, 10, 11), *weight(8, 9, 10))
-    load(*move(3, 4, 5))
-
-    def enter_encoder(g, at):
+    for g in range(3):
+        at = at_rows(g)
         x = fx[at, :] + mm(moves[2][at, :], received[0])
         fx[at, :] = x
         encoder.norm_rows(g, x, fn)
-
-    by_rows(enter_encoder)
-    encoder.project(fn)
-    encoder.attend(fine_bar, bar_k[...])
-    section = fx[...] + mm(encoder.mixed[...], encoder.wo[...])
-    fx[...] = section
-    fb[...] = section.astype(BF16)
+    encode(range(1, 3))
 
     loaded(11)
-    prepare(2, fb, moves[6])
+    prepare(2, fb[PAD:, :], moves[6])
     launch(2, onward)
+    encode(range(0, 1))
     planes[...] = mm(moves[7][...], fb[...])
     arrive(1)
     cot = cot_f[...] + mm(moves[2][...], received[1])
     cot_f[...] = cot
     out_b[...] = cot.astype(BF16)
     loaded(len(loads))
-    decoder.mixed_back(out_b, fdmixed)
     arrive(2)
     total = jnp.zeros((PAD, D), F32)
     for p in range(4):
@@ -566,9 +604,9 @@
         merged[:, lanes] = (xhat * merge_gain[:, lanes]).astype(BF16)
     cx[...] = mm(merged[...], merge_w[...])
     coarse.norm_rows(0, cx[...], cn)
-    coarse.project(cn)
-    coarse.attend(coarse_bar, bar_k[...])
-    x = cx[...] + mm(coarse.mixed[...], coarse.wo[...])
+    coarse.project(coarse.every, cn)
+    coarse.attend(coarse.every, coarse_bar, bar_k[...])
+    x = cx[...] + coarse.branch(coarse.every)
     centred = x - row_mean(x)
     rstd = lax.rsqrt(row_mean(centred * centred) + EPS)
     xhat = centred * rstd
@@ -578,35 +616,20 @@
     for p in range(4):
         fb[at_rows(p), :] = mm(cb[...], expand_w[:, at_lanes(p, D)]).astype(BF16)
 
-    prepare(3, fb, moves[9])
+    prepare(3, fb[...], moves[9])
     launch(3, back)
     fx[...] = fx[...] + mm(moves[10][...], fb[...])
+    decoder.mixed_back(decoder.every, out_b, fdmixed)
+    decode(range(0, 1))
     arrive(3)
-
-    def enter_decoder(g, at):
-        x = fx[at, :] + mm(moves[11][at, :], received[3])
-        fx[at, :] = x
-        decoder.norm_rows(g, x, fn)
-
-    by_rows(enter_decoder)
-    decoder.project(fn)
-    decoder.attend(fine_bar, bar_k[...])
-    out_b[...] = (fx[...] + mm(decoder.mixed[...], decoder.wo[...])).astype(BF16)
-
-    decoder.attend_back(fdmixed, fduq, fduk, fdqkv)
-    decoder.project_back(fduq, fduk, fdqkv, fdn)
-
-    def leave_decoder(g, at):
-        x = cot_f[at, :] + decoder.norm_backward(g, fdn[at, :])
-        gskip[at, :] = x
-        fb[at, :] = x.astype(BF16)
-
-    by_rows(leave_decoder)
-
-    prepare(5, fb, moves[6])
+    later = pl.ds(PAD, 3 * PAD)
+    fx[later, :] = fx[later, :] + mm(moves[11][later, :], received[3])
+    decode(range(1, 4))
+
+    prepare(5, fb[PAD:, :], moves[6])
     launch(5, onward)
     planes[...] = mm(moves[7][...], fb[...])
-    prepare(4, out_b, moves[3])
+    prepare(4, out_b[: 3 * PAD, :], moves[3])
     out_home[...] = mm(moves[4][...], out_b[...])
     arrive(5)
     launch(4, back)
@@ -618,9 +641,9 @@
     x = e_rstd[:, :1] * (dy - row_mean(dy) - xhat * row_mean(dy * xhat))
     cx[...] = x
     cb[...] = x.astype(BF16)
-    coarse.mixed_back(cb, cdmixed)
-    coarse.attend_back(cdmixed, cduq, cduk, cdqkv)
-    coarse.project_back(cduq, cduk, cdqkv, cdn)
+    coarse.mixed_back(coarse.every, cb, cdmixed)
+    coarse.attend_back(coarse.every, cdmixed, cduq, cduk, cdqkv)
+    coarse.project_back(coarse.every, cduq, cduk, cdqkv, cdn)
     cb[...] = (cx[...] + coarse.norm_backward(0, cdn[...])).astype(BF16)
     for p in range(4):
         planes[at_rows(p), :] = mm_nt(cb[...], merge_w[at_rows(p, D), :])
@@ -639,30 +662,26 @@
         dy = planes[at_rows(p), :] * merge_gain[:, lanes]
         fb[at_rows(p), :] = (rstd * (dy - mean - m_xhat[:, lanes] * tilt)).astype(BF16)
 
-    prepare(6, fb, moves[9])
+    prepare(6, fb[...], moves[9])
     launch(6, back)
-    gskip[...] = gskip[...] + mm(moves[10][...], fb[...])
+    x = gskip[...] + mm(moves[10][...], fb[...])
+    gskip[...] = x
+    fb[at_rows(0), :] = x[:PAD].astype(BF16)
+    encode_back(range(0, 1))
     arrive(4)
-    deliver(out_home[...] + mm(moves[5][...], received[4]), out_cells, out_hbm)
+    deliver(out_home[...] + mm(moves[5][...], received[4]), 0)
     arrive(6)
-    x = gskip[...] + mm(moves[11][...], received[6])
-    gskip[...] = x
-    fb[...] = x.astype(BF16)
-    encoder.mixed_back(fb, fdmixed)
-    encoder.attend_back(fdmixed, fduq, fduk, fdqkv)
-    encoder.project_back(fduq, fduk, fdqkv, fdn)
-
-    def leave_encoder(g, at):
-        x = gskip[at, :] + encoder.norm_backward(g, fdn[at, :])
-        fb[at, :] = x.astype(BF16)
-
-    by_rows(leave_encoder)
-
-    prepare(7, fb, moves[3])
+    x = gskip[later, :] + mm(moves[11][later, :], received[6])
+    gskip[later, :] = x
+    fb[later, :] = x.astype(BF16)
+    encode_back(range(1, 3))
+
+    prepare(7, fb[: 3 * PAD, :], moves[3])
     launch(7, back)
+    encode_back(range(3, 4))
     grad_home[...] = mm(moves[4][...], fb[...])
     arrive(7)
-    deliver(grad_home[...] + mm(moves[5][...], received[7]), grad_cells, grad_hbm)
+    deliver(grad_home[...] + mm(moves[5][...], received[7]), 1)
     for t in started:
         for copy in started[t]:
             copy.wait_send()
@@ -728,11 +747,11 @@
         pltpu.SemaphoreType.DMA((8, 3)),
         pltpu.SemaphoreType.DMA((8, 3)),
     ]
-    output, grad = pl.pallas_call(
+    results = pl.pallas_call(
         kernel,
-        out_shape=(jax.ShapeDtypeStruct(flat, BF16),) * 2,
+        out_shape=jax.ShapeDtypeStruct((2,) + flat, BF16),
         in_specs=[anywhere] * (2 + len(weights) + len(moves)) + [in_vmem] * 5 + [in_smem] * 3,
-        out_specs=(anywhere, anywhere),
+        out_specs=anywhere,
         scratch_shapes=scratch,
         compiler_params=pltpu.CompilerParams(
             collective_id=0, has_side_effects=True, vmem_limit_bytes=60 * 1024 * 1024
@@ -745,7 +764,7 @@
         *gains,
         *scales,
     )
-    return (output.astype(F32).reshape(shape), grad.astype(F32).reshape(shape))
+    return tuple(results[n].astype(F32).reshape(shape) for n in range(2))
 
 
 def solution(mesh):

time: 63.9 us -> 61.2 us (0.958)
  the two profiles are of different devices: /device:TPU:1 before, /device:TPU:6 now
where the time goes in v3:
time: 61.2 us; the launch traced here: 61.1 us
  Pallas kernels  58.3 us (95%)
  other arithmetic  2.14 us (3%)
  between operations  0.65 us (1%)
    pallas_call x1, Pallas kernels, shards(): pl.pallas_call(kernel, out_shape=jax.ShapeDtypeStruct((2,) + flat, BF16),...  58.3 us
    convert_element_type x1, other arithmetic, shards(): return tuple((results[n].astype(F32).reshape(shape) for n in range(2)))  2.14 us

profile of v3, /device:TPU:6, one launch (start us, length us, event | category | flops | bytes accessed | tf_op | source)
XLA Modules:
  0.0 61.1 jit_solution(6860214969573399208)
XLA Ops:
  0.6 58.3 %shard_map.320 = bf16[2,1152,128]{2,1,0:T(8,128)(2,1)} custom-call(f32[1152,128]{1,0:T(8,128)} %bitcast.9, f32[1152,128]{1,0:T(8,128)} %bitcast.10, bf16[512,512]{1,0:T(8,128)(2,1)} %refs_2_.1, bf16[512,1024]{1,0:T(8,128)(2,1)} %refs_3_.1, bf16[512,512]{1,0:T(8,128)(2,1)} %refs_4_.1, bf16[2048,1024]{1,0:T(8,128)(2,1)} %refs_5_.1, ...), custom_call_target="tpu_custom_call" | custom-call | tf_op jit(solution)/shard_map/pallas_call | solution.py:750
  58.9 2.1 %slice_convert_fusion = (f32[1,1152,128]{2,1,0:T(8,128)}, f32[1,1152,128]{2,1,0:T(8,128)}) fusion(bf16[2,1152,128]{2,1,0:T(8,128)(2,1)} %shard_map.320), kind=kLoop, calls=%fused_computation | loop fusion | flops 294912 | bytes 1769472 | tf_op jit(solution)/shard_map/convert_element_type | solution.py:767

commit v4 on v3

--- a/solution.py
+++ b/solution.py
@@ -149,6 +149,13 @@
     return (value * -1024).astype(F32).astype(BF16)
 
 
+def turn(src, dst):
+    rows, cols = src.shape
+    for a in range(0, rows, 256):
+        for b in range(0, cols, 256):
+            dst[pl.ds(b, 256), pl.ds(a, 256)] = src[pl.ds(a, 256), pl.ds(b, 256)].T
+
+
 class Block:
     def __init__(self, rows, channels, gain, wq, wkv, wo, scale, kept, sums):
         self.rows, self.channels = rows, channels
@@ -156,6 +163,7 @@
         self.xhat, self.rstd, self.uq, self.uk, self.rq, self.rk = kept[:6]
         self.v, self.weights, self.inverse, self.mixed = kept[6:]
         self.sums = sums
+        self.wq_t = self.wkv_t = self.wo_t = None
         self.pairs = channels // 128
         self.every = range(rows // PAD)
 
@@ -230,7 +238,11 @@
     def mixed_back(self, windows, grad_ref, dmixed_ref):
         rows = self.rows_of(windows)
         for at in self.chunks():
-            dmixed_ref[rows, at] = mm_nt(grad_ref[rows, :], self.wo[at, :]).astype(BF16)
+            if self.wo_t is None:
+                back = mm_nt(grad_ref[rows, :], self.wo[at, :])
+            else:
+                back = mm(grad_ref[rows, :], self.wo_t[:, at])
+            dmixed_ref[rows, at] = back.astype(BF16)
 
     def attend_back(self, windows, dmixed_ref, duq_ref, duk_ref, dqkv_ref):
         low = pair_masks()
@@ -279,9 +291,12 @@
                 inner = self.head_total((u * du).astype(BF16))
                 dqkv_ref[rows, to] = (r_ref[rows, at] * (du - u * inner)).astype(BF16)
         for at in self.chunks():
-            dn_ref[rows, at] = mm_nt(dqkv_ref[rows, :channels], self.wq[at, :]) + mm_nt(
-                dqkv_ref[rows, channels:], self.wkv[at, :]
-            )
+            dquery, dkeyval = dqkv_ref[rows, :channels], dqkv_ref[rows, channels:]
+            if self.wq_t is None:
+                back = mm_nt(dquery, self.wq[at, :]) + mm_nt(dkeyval, self.wkv[at, :])
+            else:
+                back = mm(dquery, self.wq_t[:, at]) + mm(dkeyval, self.wkv_t[:, at])
+            dn_ref[rows, at] = back
 
     def norm_backward(self, g, dn):
         dy = dn * self.gain[...]
@@ -355,6 +370,8 @@
         ((HOME, D), F32),
         ((HOME * 4, 128), F32),
         ((2, HOME * 4, 128), BF16),
+        ((4 * D, DC), BF16),
+        ((2 * DC, DC), BF16),
         ((2, 2 * PAD, 128), BF16),
         ((PAD, 128), BF16),
         ((256, 256), BF16),
@@ -411,7 +428,7 @@
     def move(*which):
         return [(moves_in[n], moves[n]) for n in which]
 
-    load((fields_in, fields_v), *move(0, 1), (cot_in, cot_v), *weight(0, 1, 2))
+    load((fields_in, fields_v))
 
     def device(dlat, dlon):
         return {
@@ -426,6 +443,7 @@
         pl.semaphore_signal(
             barrier, inc=1, device_id=target, device_id_type=pl.DeviceIdType.MESH
         )
+    load(*move(0, 1), (cot_in, cot_v), *weight(0, 1, 2))
 
     (
         fields_b,
@@ -446,6 +464,8 @@
         grad_home,
         by_cell,
         out_cells,
+        expand_t,
+        keyval_t,
         bar_q,
         bar_k,
         sums,
@@ -465,7 +485,8 @@
 
     def launch(t, targets):
         started[t] = []
-        for n, (start, size) in enumerate(PIECES):
+        for n in (0, 2, 1):
+            start, size = PIECES[n]
             copy = pltpu.make_async_remote_copy(
                 src_ref=sent.at[t, pl.ds(start, size)],
                 dst_ref=received.at[t, pl.ds(start, size)],
@@ -508,6 +529,9 @@
         BODY, D, dec_gain, weights[8], weights[9], weights[10], dec_scale, spaces["dec"], sums
     )
     merge_w, expand_w = weights[3], weights[7]
+    coarse.wq_t, coarse.wo_t = (expand_w.at[:, pl.ds(n * DC, DC)] for n in range(2))
+    coarse.wkv_t = keyval_t
+    merge_t = (weights[4], weights[6])
     fn, fdmixed, fduq, fduk, fdqkv, fdn, fx, fb = spaces["fine"]
     cn, cdmixed, cduq, cduk, cdqkv, cdn, cx, cb = spaces["coarse"]
 
@@ -583,7 +607,9 @@
     cot = cot_f[...] + mm(moves[2][...], received[1])
     cot_f[...] = cot
     out_b[...] = cot.astype(BF16)
-    loaded(len(loads))
+    loaded(16)
+    turn(expand_w, expand_t)
+    turn(weights[5].at[:, pl.ds(0, DC)], keyval_t.at[pl.ds(0, DC), :])
     arrive(2)
     total = jnp.zeros((PAD, D), F32)
     for p in range(4):
@@ -616,6 +642,7 @@
     for p in range(4):
         fb[at_rows(p), :] = mm(cb[...], expand_w[:, at_lanes(p, D)]).astype(BF16)
 
+    loaded(len(loads))
     prepare(3, fb[...], moves[9])
     launch(3, back)
     fx[...] = fx[...] + mm(moves[10][...], fb[...])
@@ -630,13 +657,17 @@
     launch(5, onward)
     planes[...] = mm(moves[7][...], fb[...])
     prepare(4, out_b[: 3 * PAD, :], moves[3])
-    out_home[...] = mm(moves[4][...], out_b[...])
+    turn(weights[6], coarse.wo_t)
+    turn(weights[4], coarse.wq_t)
+    turn(weights[5].at[:, pl.ds(DC, DC)], keyval_t.at[pl.ds(DC, DC), :])
+    for n in range(2):
+        turn(merge_w.at[pl.ds(n * DC, DC), :], merge_t[n])
     arrive(5)
     launch(4, back)
     for p in range(4):
         x = planes[at_rows(p), :] + mm(moves[8][at_rows(p), :], received[5])
         dexp[:, at_lanes(p, D)] = x.astype(BF16)
-    dy = mm_nt(dexp[...], expand_w[...]) * exp_gain[...]
+    dy = mm(dexp[...], expand_t[...]) * exp_gain[...]
     xhat = e_xhat[...]
     x = e_rstd[:, :1] * (dy - row_mean(dy) - xhat * row_mean(dy * xhat))
     cx[...] = x
@@ -646,7 +677,7 @@
     coarse.project_back(coarse.every, cduq, cduk, cdqkv, cdn)
     cb[...] = (cx[...] + coarse.norm_backward(0, cdn[...])).astype(BF16)
     for p in range(4):
-        planes[at_rows(p), :] = mm_nt(cb[...], merge_w[at_rows(p, D), :])
+        planes[at_rows(p), :] = mm(cb[...], merge_t[p // 2][:, at_lanes(p % 2, D)])
     total = jnp.zeros((PAD, D), F32)
     weighed = jnp.zeros((PAD, D), F32)
     for p in range(4):
@@ -667,9 +698,8 @@
     x = gskip[...] + mm(moves[10][...], fb[...])
     gskip[...] = x
     fb[at_rows(0), :] = x[:PAD].astype(BF16)
+    out_home[...] = mm(moves[4][...], out_b[...])
     encode_back(range(0, 1))
-    arrive(4)
-    deliver(out_home[...] + mm(moves[5][...], received[4]), 0)
     arrive(6)
     x = gskip[later, :] + mm(moves[11][later, :], received[6])
     gskip[later, :] = x
@@ -679,6 +709,8 @@
     prepare(7, fb[: 3 * PAD, :], moves[3])
     launch(7, back)
     encode_back(range(3, 4))
+    arrive(4)
+    deliver(out_home[...] + mm(moves[5][...], received[4]), 0)
     grad_home[...] = mm(moves[4][...], fb[...])
     arrive(7)
     deliver(grad_home[...] + mm(moves[5][...], received[7]), 1)

time: 61.2 us -> 57.8 us (0.944)
  the two profiles are of different devices: /device:TPU:6 before, /device:TPU:1 now
where the time goes in v4:
time: 57.8 us; the launch traced here: 57.6 us
  Pallas kernels  54.8 us (95%)
  other arithmetic  2.14 us (4%)
  between operations  0.65 us (1%)
    pallas_call x1, Pallas kernels, shards(): pl.pallas_call(kernel, out_shape=jax.ShapeDtypeStruct((2,) + flat, BF16),...  54.8 us
    convert_element_type x1, other arithmetic, shards(): return tuple((results[n].astype(F32).reshape(shape) for n in range(2)))  2.14 us

profile of v4, /device:TPU:1, one launch (start us, length us, event | category | flops | bytes accessed | tf_op | source)
XLA Modules:
  0.0 57.6 jit_solution(16061011179603804922)
XLA Ops:
  0.6 54.8 %shard_map.320 = bf16[2,1152,128]{2,1,0:T(8,128)(2,1)} custom-call(f32[1152,128]{1,0:T(8,128)} %bitcast.9, f32[1152,128]{1,0:T(8,128)} %bitcast.10, bf16[512,512]{1,0:T(8,128)(2,1)} %refs_2_.1, bf16[512,1024]{1,0:T(8,128)(2,1)} %refs_3_.1, bf16[512,512]{1,0:T(8,128)(2,1)} %refs_4_.1, bf16[2048,1024]{1,0:T(8,128)(2,1)} %refs_5_.1, ...), custom_call_target="tpu_custom_call" | custom-call | tf_op jit(solution)/shard_map/pallas_call | solution.py:782
  55.5 2.1 %slice_convert_fusion = (f32[1,1152,128]{2,1,0:T(8,128)}, f32[1,1152,128]{2,1,0:T(8,128)}) fusion(bf16[2,1152,128]{2,1,0:T(8,128)(2,1)} %shard_map.320), kind=kLoop, calls=%fused_computation | loop fusion | flops 294912 | bytes 1769472 | tf_op jit(solution)/shard_map/convert_element_type | solution.py:799

commit v5 on v4

--- a/solution.py
+++ b/solution.py
@@ -16,7 +16,7 @@
 PAD = 80
 BODY = 4 * PAD
 CELLS = WLAT * WLON
-PIECES = ((0, 64), (64, 64), (128, 32))
+PIECES = ((0, 64), (96, 64), (64, 32))
 SENT = 160
 D = 512
 DC = 1024
@@ -41,9 +41,9 @@
     if r >= 9 and c < 18:
         return (r - 9) * 18 + c
     if r < 9 and c >= 18:
-        return 64 + r * 6 + (c - 18)
+        return 96 + r * 6 + (c - 18)
     if r >= 9 and c >= 18:
-        return 128 + (r - 9) * 6 + (c - 18)
+        return 64 + (r - 9) * 6 + (c - 18)
     return None
 
 
@@ -206,9 +206,9 @@
             behind = pl.ds(at.start + self.channels, 512)
             self.v[rows, at] = mm(n_ref[rows, :], self.wkv[:, behind]).astype(BF16)
 
-    def scales(self, p, factor):
-        top = lax.broadcasted_iota(jnp.int32, (2 * PAD, 1), 0) < PAD
-        return jnp.where(top, self.scale[2 * p] * factor, self.scale[2 * p + 1] * factor)
+    def scaled(self, x, p, factor):
+        top, bottom = self.scale[2 * p] * factor, self.scale[2 * p + 1] * factor
+        return jnp.concatenate([x[:PAD] * top, x[PAD:] * bottom], axis=0)
 
     def attend(self, windows, barred, bar_key):
         low = pair_masks()
@@ -221,7 +221,7 @@
             for q, k, (g, p) in zip(queries, keys, units)
         ]
         weights = [
-            jnp.exp2(s * self.scales(p, LOG2E)).astype(BF16)
+            jnp.exp2(self.scaled(s, p, LOG2E)).astype(BF16)
             for s, (g, p) in zip(scores, units)
         ]
         both = [mm(w, beside(v, ones)) for w, v in zip(weights, values)]
@@ -264,7 +264,7 @@
             mm_nt(beside(d, s), beside(v, ones)) for d, s, v in zip(douts, shift, values)
         ]
         dscores = [
-            (w.astype(F32) * (d * self.scales(p, 1.0))).astype(BF16)
+            (w.astype(F32) * self.scaled(d, p, 1.0)).astype(BF16)
             for w, d, (g, p) in zip(weights, dprobs, units)
         ]
         dvalues = [mm_tn(w, d) for w, d in zip(weights, douts)]
@@ -483,9 +483,9 @@
     def prepare(t, source, pick):
         sent[t] = mm(pick[...], source).astype(BF16)
 
-    def launch(t, targets):
-        started[t] = []
-        for n in (0, 2, 1):
+    def launch(t, targets, pieces=(0, 2, 1)):
+        started.setdefault(t, [])
+        for n in pieces:
             start, size = PIECES[n]
             copy = pltpu.make_async_remote_copy(
                 src_ref=sent.at[t, pl.ds(start, size)],
@@ -498,6 +498,13 @@
             copy.start()
             started[t].append(copy)
 
+    def send(t, source, pick, targets):
+        far, near = pl.ds(0, 96), pl.ds(96, 64)
+        sent[t, far] = mm(pick[far, :], source).astype(BF16)
+        launch(t, targets, (0, 2))
+        sent[t, near] = mm(pick[near, :], source).astype(BF16)
+        launch(t, targets, (1,))
+
     def arrive(t):
         for copy in started[t]:
             copy.wait_recv()
@@ -511,13 +518,20 @@
 
     outs = []
 
-    def deliver(x, which):
-        for n in range(4):
-            by_cell[pl.ds(n, HOME, stride=4), :] = x[:, 128 * n : 128 * (n + 1)]
-        out_cells[which] = by_cell[...].astype(BF16)
-        copy = pltpu.make_async_copy(out_cells.at[which], out_hbm.at[which], out_sem.at[which])
-        copy.start()
-        outs.append(copy)
+    def deliver(own, t, which):
+        half = HOME // 2
+        for h in range(2):
+            rows, cells = pl.ds(h * half, half), pl.ds(4 * h * half, 4 * half)
+            x = own[rows, :] + mm(moves[5][rows, :], received[t])
+            for n in range(4):
+                at = pl.ds(4 * h * half + n, half, stride=4)
+                by_cell[at, :] = x[:, 128 * n : 128 * (n + 1)]
+            out_cells[which, cells] = by_cell[cells, :].astype(BF16)
+            copy = pltpu.make_async_copy(
+                out_cells.at[which, cells], out_hbm.at[which, cells], out_sem.at[which, h]
+            )
+            copy.start()
+            outs.append(copy)
 
     encoder = Block(
         BODY, D, enc_gain, weights[0], weights[1], weights[2], enc_scale, spaces["enc"], sums
@@ -591,16 +605,20 @@
     loaded(8)
     arrive(0)
     launch(1, onward)
-    for g in range(3):
+
+    def enter_encoder(g):
         at = at_rows(g)
         x = fx[at, :] + mm(moves[2][at, :], received[0])
         fx[at, :] = x
         encoder.norm_rows(g, x, fn)
+
+    enter_encoder(1)
+    enter_encoder(2)
     encode(range(1, 3))
 
     loaded(11)
-    prepare(2, fb[PAD:, :], moves[6])
-    launch(2, onward)
+    send(2, fb[PAD:, :], moves[6], onward)
+    enter_encoder(0)
     encode(range(0, 1))
     planes[...] = mm(moves[7][...], fb[...])
     arrive(1)
@@ -643,8 +661,7 @@
         fb[at_rows(p), :] = mm(cb[...], expand_w[:, at_lanes(p, D)]).astype(BF16)
 
     loaded(len(loads))
-    prepare(3, fb[...], moves[9])
-    launch(3, back)
+    send(3, fb[...], moves[9], back)
     fx[...] = fx[...] + mm(moves[10][...], fb[...])
     decoder.mixed_back(decoder.every, out_b, fdmixed)
     decode(range(0, 1))
@@ -653,8 +670,7 @@
     fx[later, :] = fx[later, :] + mm(moves[11][later, :], received[3])
     decode(range(1, 4))
 
-    prepare(5, fb[PAD:, :], moves[6])
-    launch(5, onward)
+    send(5, fb[PAD:, :], moves[6], onward)
     planes[...] = mm(moves[7][...], fb[...])
     prepare(4, out_b[: 3 * PAD, :], moves[3])
     turn(weights[6], coarse.wo_t)
@@ -693,27 +709,31 @@
         dy = planes[at_rows(p), :] * merge_gain[:, lanes]
         fb[at_rows(p), :] = (rstd * (dy - mean - m_xhat[:, lanes] * tilt)).astype(BF16)
 
-    prepare(6, fb[...], moves[9])
-    launch(6, back)
+    send(6, fb[...], moves[9], back)
     x = gskip[...] + mm(moves[10][...], fb[...])
     gskip[...] = x
     fb[at_rows(0), :] = x[:PAD].astype(BF16)
     out_home[...] = mm(moves[4][...], out_b[...])
     encode_back(range(0, 1))
     arrive(6)
-    x = gskip[later, :] + mm(moves[11][later, :], received[6])
-    gskip[later, :] = x
-    fb[later, :] = x.astype(BF16)
+
+    def enter_gradient(windows):
+        at = encoder.rows_of(windows)
+        x = gskip[at, :] + mm(moves[11][at, :], received[6])
+        gskip[at, :] = x
+        fb[at, :] = x.astype(BF16)
+
+    enter_gradient(range(1, 3))
     encode_back(range(1, 3))
 
-    prepare(7, fb[: 3 * PAD, :], moves[3])
-    launch(7, back)
+    send(7, fb[: 3 * PAD, :], moves[3], back)
+    enter_gradient(range(3, 4))
     encode_back(range(3, 4))
     arrive(4)
-    deliver(out_home[...] + mm(moves[5][...], received[4]), 0)
+    deliver(out_home, 4, 0)
     grad_home[...] = mm(moves[4][...], fb[...])
     arrive(7)
-    deliver(grad_home[...] + mm(moves[5][...], received[7]), 1)
+    deliver(grad_home, 7, 1)
     for t in started:
         for copy in started[t]:
             copy.wait_send()
@@ -775,7 +795,7 @@
         scratch += [pltpu.VMEM(s, t) for s, t in TABLE[name]]
     scratch += [
         pltpu.SemaphoreType.DMA((2 + len(weights) + len(moves),)),
-        pltpu.SemaphoreType.DMA((2,)),
+        pltpu.SemaphoreType.DMA((2, 2)),
         pltpu.SemaphoreType.DMA((8, 3)),
         pltpu.SemaphoreType.DMA((8, 3)),
     ]

time: 57.8 us -> 57.8 us (level)
  no operation moved by 1% of the time
where the time goes in v5:
time: 57.8 us; the launch traced here: 57.6 us
  Pallas kernels  54.8 us (95%)
  other arithmetic  2.14 us (4%)
  between operations  0.65 us (1%)
    pallas_call x1, Pallas kernels, shards(): pl.pallas_call(kernel, out_shape=jax.ShapeDtypeStruct((2,) + flat, BF16),...  54.8 us
    convert_element_type x1, other arithmetic, shards(): return tuple((results[n].astype(F32).reshape(shape) for n in range(2)))  2.14 us

profile of v5, /device:TPU:1, one launch (start us, length us, event | category | flops | bytes accessed | tf_op | source)
XLA Modules:
  0.0 57.6 jit_solution(13666994365126376161)
XLA Ops:
  0.6 54.8 %shard_map.320 = bf16[2,1152,128]{2,1,0:T(8,128)(2,1)} custom-call(f32[1152,128]{1,0:T(8,128)} %bitcast.9, f32[1152,128]{1,0:T(8,128)} %bitcast.10, bf16[512,512]{1,0:T(8,128)(2,1)} %refs_2_.1, bf16[512,1024]{1,0:T(8,128)(2,1)} %refs_3_.1, bf16[512,512]{1,0:T(8,128)(2,1)} %refs_4_.1, bf16[2048,1024]{1,0:T(8,128)(2,1)} %refs_5_.1, ...), custom_call_target="tpu_custom_call" | custom-call | tf_op jit(solution)/shard_map/pallas_call | solution.py:802
  55.5 2.1 %slice_convert_fusion = (f32[1,1152,128]{2,1,0:T(8,128)}, f32[1,1152,128]{2,1,0:T(8,128)}) fusion(bf16[2,1152,128]{2,1,0:T(8,128)(2,1)} %shard_map.320), kind=kLoop, calls=%fused_computation | loop fusion | flops 294912 | bytes 1769472 | tf_op jit(solution)/shard_map/convert_element_type | solution.py:819

commit v6 on v5

--- a/solution.py
+++ b/solution.py
@@ -604,7 +604,6 @@
     encode(range(3, 4))
     loaded(8)
     arrive(0)
-    launch(1, onward)
 
     def enter_encoder(g):
         at = at_rows(g)
@@ -621,14 +620,11 @@
     enter_encoder(0)
     encode(range(0, 1))
     planes[...] = mm(moves[7][...], fb[...])
-    arrive(1)
-    cot = cot_f[...] + mm(moves[2][...], received[1])
-    cot_f[...] = cot
-    out_b[...] = cot.astype(BF16)
     loaded(16)
     turn(expand_w, expand_t)
     turn(weights[5].at[:, pl.ds(0, DC)], keyval_t.at[pl.ds(0, DC), :])
     arrive(2)
+    launch(1, onward)
     total = jnp.zeros((PAD, D), F32)
     for p in range(4):
         x = planes[at_rows(p), :] + mm(moves[8][at_rows(p), :], received[2])
@@ -663,6 +659,10 @@
     loaded(len(loads))
     send(3, fb[...], moves[9], back)
     fx[...] = fx[...] + mm(moves[10][...], fb[...])
+    arrive(1)
+    cot = cot_f[...] + mm(moves[2][...], received[1])
+    cot_f[...] = cot
+    out_b[...] = cot.astype(BF16)
     decoder.mixed_back(decoder.every, out_b, fdmixed)
     decode(range(0, 1))
     arrive(3)
@@ -715,6 +715,11 @@
     fb[at_rows(0), :] = x[:PAD].astype(BF16)
     out_home[...] = mm(moves[4][...], out_b[...])
     encode_back(range(0, 1))
+    encoder.wq_t, encoder.wo_t = weights[8], weights[10]
+    encoder.wkv_t = keyval_t.at[pl.ds(0, 2 * D), pl.ds(0, D)]
+    turn(weights[0], encoder.wq_t)
+    turn(weights[1], encoder.wkv_t)
+    turn(weights[2], encoder.wo_t)
     arrive(6)
 
     def enter_gradient(windows):

time: 57.8 us -> 56.1 us (0.971)
  Pallas kernels: 54.8 us -> 53 us
    pallas_call x1, Pallas kernels: 54.8 us -> 53 us  [shards(): pl.pallas_call(kernel, out_shape=jax.ShapeDtypeStruct((2,) + flat, BF16),...]
where the time goes in v6:
time: 56.1 us; the launch traced here: 55.8 us
  Pallas kernels  53 us (94%)
  other arithmetic  2.14 us (4%)
  between operations  0.65 us (1%)
    pallas_call x1, Pallas kernels, shards(): pl.pallas_call(kernel, out_shape=jax.ShapeDtypeStruct((2,) + flat, BF16),...  53 us
    convert_element_type x1, other arithmetic, shards(): return tuple((results[n].astype(F32).reshape(shape) for n in range(2)))  2.14 us

profile of v6, /device:TPU:1, one launch (start us, length us, event | category | flops | bytes accessed | tf_op | source)
XLA Modules:
  0.0 55.8 jit_solution(5184098136390350002)
XLA Ops:
  0.6 53.0 %shard_map.320 = bf16[2,1152,128]{2,1,0:T(8,128)(2,1)} custom-call(f32[1152,128]{1,0:T(8,128)} %bitcast.9, f32[1152,128]{1,0:T(8,128)} %bitcast.10, bf16[512,512]{1,0:T(8,128)(2,1)} %refs_2_.1, bf16[512,1024]{1,0:T(8,128)(2,1)} %refs_3_.1, bf16[512,512]{1,0:T(8,128)(2,1)} %refs_4_.1, bf16[2048,1024]{1,0:T(8,128)(2,1)} %refs_5_.1, ...), custom_call_target="tpu_custom_call" | custom-call | tf_op jit(solution)/shard_map/pallas_call | solution.py:807
  53.7 2.1 %slice_convert_fusion = (f32[1,1152,128]{2,1,0:T(8,128)}, f32[1,1152,128]{2,1,0:T(8,128)}) fusion(bf16[2,1152,128]{2,1,0:T(8,128)(2,1)} %shard_map.320), kind=kLoop, calls=%fused_computation | loop fusion | flops 294912 | bytes 1769472 | tf_op jit(solution)/shard_map/convert_element_type | solution.py:824

commit v7 on v6

--- a/solution.py
+++ b/solution.py
@@ -564,12 +564,10 @@
         fb[rows, :] = section.astype(BF16)
 
     def decode(windows):
-        rows = decoder.rows_of(windows)
         for g in windows:
             decoder.norm_rows(g, fx[at_rows(g), :], fn)
         decoder.project(windows, fn)
         decoder.attend(windows, fine_bar, bar_k[...])
-        out_b[rows, :] = (fx[rows, :] + decoder.branch(windows)).astype(BF16)
         decoder.attend_back(windows, fdmixed, fduq, fduk, fdqkv)
         decoder.project_back(windows, fduq, fduk, fdqkv, fdn)
         for g in windows:
@@ -672,6 +670,7 @@
 
     send(5, fb[PAD:, :], moves[6], onward)
     planes[...] = mm(moves[7][...], fb[...])
+    out_b[...] = (fx[...] + decoder.branch(decoder.every)).astype(BF16)
     prepare(4, out_b[: 3 * PAD, :], moves[3])
     turn(weights[6], coarse.wo_t)
     turn(weights[4], coarse.wq_t)

time: 56.1 us -> 55.9 us (level)
  no operation moved by 1% of the time
where the time goes in v7:
time: 55.9 us; the launch traced here: 55.7 us
  Pallas kernels  52.9 us (95%)
  other arithmetic  2.14 us (4%)
  between operations  0.65 us (1%)
    pallas_call x1, Pallas kernels, shards(): pl.pallas_call(kernel, out_shape=jax.ShapeDtypeStruct((2,) + flat, BF16),...  52.9 us
    convert_element_type x1, other arithmetic, shards(): return tuple((results[n].astype(F32).reshape(shape) for n in range(2)))  2.14 us

profile of v7, /device:TPU:1, one launch (start us, length us, event | category | flops | bytes accessed | tf_op | source)
XLA Modules:
  0.0 55.7 jit_solution(393226680175915003)
XLA Ops:
  0.6 52.9 %shard_map.320 = bf16[2,1152,128]{2,1,0:T(8,128)(2,1)} custom-call(f32[1152,128]{1,0:T(8,128)} %bitcast.9, f32[1152,128]{1,0:T(8,128)} %bitcast.10, bf16[512,512]{1,0:T(8,128)(2,1)} %refs_2_.1, bf16[512,1024]{1,0:T(8,128)(2,1)} %refs_3_.1, bf16[512,512]{1,0:T(8,128)(2,1)} %refs_4_.1, bf16[2048,1024]{1,0:T(8,128)(2,1)} %refs_5_.1, ...), custom_call_target="tpu_custom_call" | custom-call | tf_op jit(solution)/shard_map/pallas_call | solution.py:806
  53.6 2.1 %slice_convert_fusion = (f32[1,1152,128]{2,1,0:T(8,128)}, f32[1,1152,128]{2,1,0:T(8,128)}) fusion(bf16[2,1152,128]{2,1,0:T(8,128)(2,1)} %shard_map.320), kind=kLoop, calls=%fused_computation | loop fusion | flops 294912 | bytes 1769472 | tf_op jit(solution)/shard_map/convert_element_type | solution.py:823
